TPU v7x, 512 devices: a whole 4x8x8 slice. The times are simulated.
512 devices in a mesh: row: 32 (over z, x), col: 8 (over y), layer: 2 (over core).
Axes of the slice: x: 4, y: 8, z: 8, core: 2. Of those that a mesh axis runs over, the one named last changes fastest.
Arguments:
- blocks: bfloat16 [1536, 12, 128, 128], P(('row', 'col', 'layer')), may hold values from -0.75 to 0.75
- block_rows: int32 [1536, 12], P(('row', 'col', 'layer')), may hold values from 0 to 1535, as said below
Outputs:
- refined: bfloat16 [1536, 12, 128, 128], P(('row', 'col', 'layer'))
Inputs may be any that keep to these rules, and one draw needn't show every extreme that they name: `block_rows`: in block column c the 12 entries are distinct, include c itself, and each equals (c + d) mod 1536 with -8 <= d <= 8.
All inputs are finite; a program needn't handle non-finite values.
Results may differ from a plain program's by a relative error of at most 0.0049.
Values may be sent and summed in bfloat16 or wider, within the bound.
No kernel may reach another device: no remote copies, remote signals or barrier semaphores. Data moves between devices by JAX's collectives and lax.ppermute only.
A program may use at most 64 MiB of HBM per device.

v0:
```python
import jax
import jax.numpy as jnp
from jax import lax
from jax.sharding import PartitionSpec as P

BAND = 8


def passed_along(value, axis, steps):
    count = lax.axis_size(axis)
    pairs = [(source, (source + steps) % count) for source in range(count)]
    return lax.ppermute(value, axis, pairs)


def multiply(near_blocks, near_lists, near_index, block_rows, right):
    col_count = block_rows.shape[0]
    slot_count = block_rows.shape[1]
    tile_size = near_blocks.shape[2]
    flattened = near_blocks.reshape(-1, tile_size, tile_size)
    their_rows = near_lists[near_index]
    slot_ids = jnp.arange(slot_count, dtype=jnp.int32)[None, None, :]

    def one_slot(slot_index, running):
        wanted = lax.dynamic_index_in_dim(block_rows, slot_index, 1, keepdims=False)
        matches = their_rows == wanted[:, None, None]
        position = jnp.sum(jnp.where(matches, slot_ids, 0), axis=2)
        present = jnp.any(matches, axis=2)
        selected = flattened[near_index * slot_count + position]
        selected = jnp.where(present[..., None, None], selected, jnp.zeros((), selected.dtype))
        term = jnp.einsum("cknm,ckmq->cnq", selected, right, preferred_element_type=jnp.float32)
        return lax.dynamic_update_index_in_dim(running, term, slot_index, 1)

    running = jnp.zeros((col_count, slot_count, tile_size, tile_size), jnp.float32)
    return lax.fori_loop(0, slot_count, one_slot, running)


def shards(blocks, block_rows):
    col_count = blocks.shape[0]
    column_total = col_count * lax.axis_size(("row", "col", "layer"))
    own_columns = lax.axis_index(("row", "col", "layer")) * col_count + jnp.arange(
        col_count, dtype=jnp.int32
    )
    pieces = []
    list_pieces = []
    reach_steps = (BAND + col_count - 1) // col_count
    for offset_step in (
        list(range(reach_steps, 0, -1)) + [0] + list(range(-1, -reach_steps - 1, -1))
    ):
        if offset_step == 0:
            pieces.append(blocks)
            list_pieces.append(block_rows)
        else:
            moved_blocks, moved_lists = passed_along(
                (blocks, block_rows), ("row", "col", "layer"), offset_step
            )
            pieces.append(moved_blocks)
            list_pieces.append(moved_lists)
    near_base = reach_steps * col_count
    near_blocks = jnp.concatenate(pieces, axis=0)
    near_lists = jnp.concatenate(list_pieces, axis=0)
    distance = (
        block_rows - own_columns[:, None] + column_total // 2
    ) % column_total - column_total // 2
    near_index = near_base + jnp.arange(col_count, dtype=jnp.int32)[:, None] + distance
    square = multiply(near_blocks, near_lists, near_index, block_rows, blocks).astype(jnp.bfloat16)
    cubed = multiply(near_blocks, near_lists, near_index, block_rows, square)
    return (3.0 * square.astype(jnp.float32) - 2.0 * cubed).astype(jnp.bfloat16)


def solution(mesh):
    placed = (P(("row", "col", "layer"), None, None, None), P(("row", "col", "layer"), None))
    return jax.shard_map(
        shards,
        mesh=mesh,
        in_specs=placed,
        out_specs=P(("row", "col", "layer"), None, None, None),
        check_vma=False,
    )
```

profile of v0, /device:TPU:1, one launch (start us, length us, event | category | flops | bytes accessed | tf_op | source)
XLA Modules:
  0.0 363.5 jit_solution(10048925833880215148)
XLA Ops:
  0.0 5.7 %collective-permute-start.6 = (bf16[3,12,128,128]{3,2,1,0:T(8,128)(2,1)}, bf16[3,12,128,128]{3,2,1,0:T(8,128)(2,1)S(1)}, u32[]{:S(2)}, u32[]{:S(2)}) collective-permute-start(bf16[3,12,128,128]{3,2,1,0:T(8,128)(2,1)} %param.6), channel_id=1, source_target_pairs={{0,3},{1,4},{2,5},{3,6},{4,7},{5,8},{6,9},{7,10},{8,11},{9,12},{10... | collective-permute-start | bytes 3538952 | tf_op jit(solution)/shard_map/ppermute | solution.py:12
  5.7 3.2 collective-permute-start.7
  9.0 2.2 collective-permute-start.8
  11.2 3.5 collective-permute-start.9
  14.7 4.2 %collective-permute-start = (s32[3,12]{1,0:T(4,128)}, s32[3,12]{1,0:T(4,128)S(1)}, u32[]{:S(2)}, u32[]{:S(2)}) collective-permute-start(s32[3,12]{1,0:T(4,128)} %param.7), channel_id=1, source_target_pairs={{0,3},{1,4},{2,5},{3,6},{4,7},{5,8},{6,9},{7,10},{8,11},{9,12},{10... | collective-permute-start | bytes 440 | tf_op jit(solution)/shard_map/ppermute | solution.py:12
  19.0 63.5 %collective-permute-done = s32[3,12]{1,0:T(4,128)S(1)} collective-permute-done((s32[3,12]{1,0:T(4,128)}, s32[3,12]{1,0:T(4,128)S(1)}, u32[]{:S(2)}, u32[]{:S(2)}) %collective-permute-start) | collective-permute-done | bytes 176 | tf_op jit(solution)/shard_map/ppermute | solution.py:12
  82.5 2.3 collective-permute-start.1
  84.7 11.7 %collective-permute-done.1 = s32[3,12]{1,0:T(4,128)S(1)} collective-permute-done((s32[3,12]{1,0:T(4,128)}, s32[3,12]{1,0:T(4,128)S(1)}, u32[]{:S(2)}, u32[]{:S(2)}) %collective-permute-start.1) | collective-permute-done | bytes 176 | tf_op jit(solution)/shard_map/ppermute | solution.py:12
  96.5 6.6 %collective-permute-start.2 = (s32[3,12]{1,0:T(4,128)}, s32[3,12]{1,0:T(4,128)S(1)}, u32[]{:S(2)}, u32[]{:S(2)}) collective-permute-start(s32[3,12]{1,0:T(4,128)} %param.7), channel_id=1, source_target_pairs={{0,1},{1,2},{2,3},{3,4},{4,5},{5,6},{6,7},{7,8},{8,9},{9,10},{10,1... | collective-permute-start | bytes 440 | tf_op jit(solution)/shard_map/ppermute | solution.py:12
  103.1 6.0 %collective-permute-done.2 = s32[3,12]{1,0:T(4,128)S(1)} collective-permute-done((s32[3,12]{1,0:T(4,128)}, s32[3,12]{1,0:T(4,128)S(1)}, u32[]{:S(2)}, u32[]{:S(2)}) %collective-permute-start.2) | collective-permute-done | bytes 176 | tf_op jit(solution)/shard_map/ppermute | solution.py:12
  109.1 9.7 %collective-permute-start.3 = (s32[3,12]{1,0:T(4,128)}, s32[3,12]{1,0:T(4,128)S(1)}, u32[]{:S(2)}, u32[]{:S(2)}) collective-permute-start(s32[3,12]{1,0:T(4,128)} %param.7), channel_id=1, source_target_pairs={{0,511},{1,0},{2,1},{3,2},{4,3},{5,4},{6,5},{7,6},{8,7},{9,8},{10,... | collective-permute-start | bytes 440 | tf_op jit(solution)/shard_map/ppermute | solution.py:12
  119.8 9.1 %collective-permute-start.4 = (s32[3,12]{1,0:T(4,128)}, s32[3,12]{1,0:T(4,128)S(1)}, u32[]{:S(2)}, u32[]{:S(2)}) collective-permute-start(s32[3,12]{1,0:T(4,128)} %param.7), channel_id=1, source_target_pairs={{0,510},{1,511},{2,0},{3,1},{4,2},{5,3},{6,4},{7,5},{8,6},{9,7},{1... | collective-permute-start | bytes 440 | tf_op jit(solution)/shard_map/ppermute | solution.py:12
  129.9 3.1 collective-permute-start.5
  133.0 3.0 collective-permute-done.5
  136.0 14.4 %collective-permute-start.10 = (bf16[3,12,128,128]{3,2,1,0:T(8,128)(2,1)}, bf16[3,12,128,128]{3,2,1,0:T(8,128)(2,1)}, u32[]{:S(2)}, u32[]{:S(2)}) collective-permute-start(bf16[3,12,128,128]{3,2,1,0:T(8,128)(2,1)} %param.6), channel_id=1, source_target_pairs={{0,510},{1,511},{2,0},{3,1},{4,2},{5,3},{6,4},{7,5},{8,6},{9,7},{1... | collective-permute-start | bytes 3538952 | tf_op jit(solution)/shard_map/ppermute | solution.py:12
  150.5 1.9 collective-permute-start.11
  160.0 19.8 %collective-permute-done.10 = bf16[3,12,128,128]{3,2,1,0:T(8,128)(2,1)} collective-permute-done((bf16[3,12,128,128]{3,2,1,0:T(8,128)(2,1)}, bf16[3,12,128,128]{3,2,1,0:T(8,128)(2,1)}, u32[]{:S(2)}, u32[]{:S(2)}) %collective-permute-start.10) | collective-permute-done | bytes 1179680 | tf_op jit(solution)/shard_map/ppermute | solution.py:12
  181.3 26.8 %collective-permute-done.11 = bf16[3,12,128,128]{3,2,1,0:T(8,128)(2,1)} collective-permute-done((bf16[3,12,128,128]{3,2,1,0:T(8,128)(2,1)}, bf16[3,12,128,128]{3,2,1,0:T(8,128)(2,1)}, u32[]{:S(2)}, u32[]{:S(2)}) %collective-permute-start.11) | collective-permute-done | bytes 1179680 | tf_op jit(solution)/shard_map/ppermute | solution.py:12
  209.6 3.2 copy-done
  212.7 77.7 %while.30 = (s32[]{:T(128)}, bf16[3,12,128,128]{3,2,1,0:T(8,128)(2,1)S(1)}, s32[3,12]{0,1:T(8,128)S(1)}, s32[3,12,12]{2,1,0:T(8,128)S(1)}, s32[3,12]{1,0:T(4,128...) while((s32[]{:T(128)}, ...), condition=%wide.region_3.4_spmd.clone.clone, body=%wide.region_0.3_spmd.clone.sunk.clone | while | flops 151587632 | bytes 4923709 | solution.py:34
  213.2 4.1 %gather_fusion = bf16[36,128,128]{2,1,0:T(8,128)(2,1)S(1)} fusion(bf16[252,128,128]{2,1,0:T(8,128)(2,1)} %get-tuple-element.530, s32[1024]{0:T(1024)S(1)} %pad_clamp_fusion.7), kind=kCustom, calls=%fused_computation.clone.clone.1.clone | custom fusion | bytes 2359440 | tf_op jit(solution)/shard_map/while/body/eval_jaxpr/gather | solution.py:28
  217.3 1.8 fusion.59
  219.7 4.1 %gather_fusion = bf16[36,128,128]{2,1,0:T(8,128)(2,1)S(1)} fusion(bf16[252,128,128]{2,1,0:T(8,128)(2,1)} %get-tuple-element.530, s32[1024]{0:T(1024)S(1)} %pad_clamp_fusion.7), kind=kCustom, calls=%fused_computation.clone.clone.1.clone | custom fusion | bytes 2359440 | tf_op jit(solution)/shard_map/while/body/eval_jaxpr/gather | solution.py:28
  226.2 4.1 %gather_fusion = bf16[36,128,128]{2,1,0:T(8,128)(2,1)S(1)} fusion(bf16[252,128,128]{2,1,0:T(8,128)(2,1)} %get-tuple-element.530, s32[1024]{0:T(1024)S(1)} %pad_clamp_fusion.7), kind=kCustom, calls=%fused_computation.clone.clone.1.clone | custom fusion | bytes 2359440 | tf_op jit(solution)/shard_map/while/body/eval_jaxpr/gather | solution.py:28
  230.3 1.8 fusion.59
  232.6 4.1 %gather_fusion = bf16[36,128,128]{2,1,0:T(8,128)(2,1)S(1)} fusion(bf16[252,128,128]{2,1,0:T(8,128)(2,1)} %get-tuple-element.530, s32[1024]{0:T(1024)S(1)} %pad_clamp_fusion.7), kind=kCustom, calls=%fused_computation.clone.clone.1.clone | custom fusion | bytes 2359440 | tf_op jit(solution)/shard_map/while/body/eval_jaxpr/gather | solution.py:28
  239.1 4.1 %gather_fusion = bf16[36,128,128]{2,1,0:T(8,128)(2,1)S(1)} fusion(bf16[252,128,128]{2,1,0:T(8,128)(2,1)} %get-tuple-element.530, s32[1024]{0:T(1024)S(1)} %pad_clamp_fusion.7), kind=kCustom, calls=%fused_computation.clone.clone.1.clone | custom fusion | bytes 2359440 | tf_op jit(solution)/shard_map/while/body/eval_jaxpr/gather | solution.py:28
  245.6 4.1 %gather_fusion = bf16[36,128,128]{2,1,0:T(8,128)(2,1)S(1)} fusion(bf16[252,128,128]{2,1,0:T(8,128)(2,1)} %get-tuple-element.530, s32[1024]{0:T(1024)S(1)} %pad_clamp_fusion.7), kind=kCustom, calls=%fused_computation.clone.clone.1.clone | custom fusion | bytes 2359440 | tf_op jit(solution)/shard_map/while/body/eval_jaxpr/gather | solution.py:28
  252.1 4.1 %gather_fusion = bf16[36,128,128]{2,1,0:T(8,128)(2,1)S(1)} fusion(bf16[252,128,128]{2,1,0:T(8,128)(2,1)} %get-tuple-element.530, s32[1024]{0:T(1024)S(1)} %pad_clamp_fusion.7), kind=kCustom, calls=%fused_computation.clone.clone.1.clone | custom fusion | bytes 2359440 | tf_op jit(solution)/shard_map/while/body/eval_jaxpr/gather | solution.py:28
  258.6 4.1 %gather_fusion = bf16[36,128,128]{2,1,0:T(8,128)(2,1)S(1)} fusion(bf16[252,128,128]{2,1,0:T(8,128)(2,1)} %get-tuple-element.530, s32[1024]{0:T(1024)S(1)} %pad_clamp_fusion.7), kind=kCustom, calls=%fused_computation.clone.clone.1.clone | custom fusion | bytes 2359440 | tf_op jit(solution)/shard_map/while/body/eval_jaxpr/gather | solution.py:28
  265.0 4.1 %gather_fusion = bf16[36,128,128]{2,1,0:T(8,128)(2,1)S(1)} fusion(bf16[252,128,128]{2,1,0:T(8,128)(2,1)} %get-tuple-element.530, s32[1024]{0:T(1024)S(1)} %pad_clamp_fusion.7), kind=kCustom, calls=%fused_computation.clone.clone.1.clone | custom fusion | bytes 2359440 | tf_op jit(solution)/shard_map/while/body/eval_jaxpr/gather | solution.py:28
  271.5 4.1 %gather_fusion = bf16[36,128,128]{2,1,0:T(8,128)(2,1)S(1)} fusion(bf16[252,128,128]{2,1,0:T(8,128)(2,1)} %get-tuple-element.530, s32[1024]{0:T(1024)S(1)} %pad_clamp_fusion.7), kind=kCustom, calls=%fused_computation.clone.clone.1.clone | custom fusion | bytes 2359440 | tf_op jit(solution)/shard_map/while/body/eval_jaxpr/gather | solution.py:28
  278.0 4.1 %gather_fusion = bf16[36,128,128]{2,1,0:T(8,128)(2,1)S(1)} fusion(bf16[252,128,128]{2,1,0:T(8,128)(2,1)} %get-tuple-element.530, s32[1024]{0:T(1024)S(1)} %pad_clamp_fusion.7), kind=kCustom, calls=%fused_computation.clone.clone.1.clone | custom fusion | bytes 2359440 | tf_op jit(solution)/shard_map/while/body/eval_jaxpr/gather | solution.py:28
  284.5 4.1 %gather_fusion = bf16[36,128,128]{2,1,0:T(8,128)(2,1)S(1)} fusion(bf16[252,128,128]{2,1,0:T(8,128)(2,1)} %get-tuple-element.530, s32[1024]{0:T(1024)S(1)} %pad_clamp_fusion.7), kind=kCustom, calls=%fused_computation.clone.clone.1.clone | custom fusion | bytes 2359440 | tf_op jit(solution)/shard_map/while/body/eval_jaxpr/gather | solution.py:28
  290.4 70.0 %while.31 = (s32[]{:T(128)}, f32[3,12,128,128]{3,2,1,0:T(8,128)}, s32[3,12]{0,1:T(8,128)S(1)}, s32[3,12,12]{2,1,0:T(8,128)S(1)}, s32[3,12]{1,0:T(4,128)S(1)}, /*...) while((s32[]{:T(128)}, f32[3,12,128,128]{3,2,1,0:T(8,128)}, ...), condition=%wide.region_7.8_spmd.clone.clone, body=%wide.region_4.7_spmd.clone.sunk.clone | while | flops 151587632 | bytes 4923741 | solution.py:34
  290.9 4.1 %gather_fusion.1 = bf16[36,128,128]{2,1,0:T(8,128)(2,1)S(1)} fusion(bf16[252,128,128]{2,1,0:T(8,128)(2,1)} %get-tuple-element.551, s32[1024]{0:T(1024)S(1)} %pad_clamp_fusion.8), kind=kCustom, calls=%fused_computation.1.clone.clone.1.clone | custom fusion | bytes 2359440 | tf_op jit(solution)/shard_map/while/body/eval_jaxpr/gather | solution.py:28
  296.8 4.1 %gather_fusion.1 = bf16[36,128,128]{2,1,0:T(8,128)(2,1)S(1)} fusion(bf16[252,128,128]{2,1,0:T(8,128)(2,1)} %get-tuple-element.551, s32[1024]{0:T(1024)S(1)} %pad_clamp_fusion.8), kind=kCustom, calls=%fused_computation.1.clone.clone.1.clone | custom fusion | bytes 2359440 | tf_op jit(solution)/shard_map/while/body/eval_jaxpr/gather | solution.py:28
  302.6 4.1 %gather_fusion.1 = bf16[36,128,128]{2,1,0:T(8,128)(2,1)S(1)} fusion(bf16[252,128,128]{2,1,0:T(8,128)(2,1)} %get-tuple-element.551, s32[1024]{0:T(1024)S(1)} %pad_clamp_fusion.8), kind=kCustom, calls=%fused_computation.1.clone.clone.1.clone | custom fusion | bytes 2359440 | tf_op jit(solution)/shard_map/while/body/eval_jaxpr/gather | solution.py:28
  308.4 4.1 %gather_fusion.1 = bf16[36,128,128]{2,1,0:T(8,128)(2,1)S(1)} fusion(bf16[252,128,128]{2,1,0:T(8,128)(2,1)} %get-tuple-element.551, s32[1024]{0:T(1024)S(1)} %pad_clamp_fusion.8), kind=kCustom, calls=%fused_computation.1.clone.clone.1.clone | custom fusion | bytes 2359440 | tf_op jit(solution)/shard_map/while/body/eval_jaxpr/gather | solution.py:28
  314.3 4.1 %gather_fusion.1 = bf16[36,128,128]{2,1,0:T(8,128)(2,1)S(1)} fusion(bf16[252,128,128]{2,1,0:T(8,128)(2,1)} %get-tuple-element.551, s32[1024]{0:T(1024)S(1)} %pad_clamp_fusion.8), kind=kCustom, calls=%fused_computation.1.clone.clone.1.clone | custom fusion | bytes 2359440 | tf_op jit(solution)/shard_map/while/body/eval_jaxpr/gather | solution.py:28
  320.1 4.1 %gather_fusion.1 = bf16[36,128,128]{2,1,0:T(8,128)(2,1)S(1)} fusion(bf16[252,128,128]{2,1,0:T(8,128)(2,1)} %get-tuple-element.551, s32[1024]{0:T(1024)S(1)} %pad_clamp_fusion.8), kind=kCustom, calls=%fused_computation.1.clone.clone.1.clone | custom fusion | bytes 2359440 | tf_op jit(solution)/shard_map/while/body/eval_jaxpr/gather | solution.py:28
  325.9 4.1 %gather_fusion.1 = bf16[36,128,128]{2,1,0:T(8,128)(2,1)S(1)} fusion(bf16[252,128,128]{2,1,0:T(8,128)(2,1)} %get-tuple-element.551, s32[1024]{0:T(1024)S(1)} %pad_clamp_fusion.8), kind=kCustom, calls=%fused_computation.1.clone.clone.1.clone | custom fusion | bytes 2359440 | tf_op jit(solution)/shard_map/while/body/eval_jaxpr/gather | solution.py:28
  331.8 4.1 %gather_fusion.1 = bf16[36,128,128]{2,1,0:T(8,128)(2,1)S(1)} fusion(bf16[252,128,128]{2,1,0:T(8,128)(2,1)} %get-tuple-element.551, s32[1024]{0:T(1024)S(1)} %pad_clamp_fusion.8), kind=kCustom, calls=%fused_computation.1.clone.clone.1.clone | custom fusion | bytes 2359440 | tf_op jit(solution)/shard_map/while/body/eval_jaxpr/gather | solution.py:28
  337.6 4.1 %gather_fusion.1 = bf16[36,128,128]{2,1,0:T(8,128)(2,1)S(1)} fusion(bf16[252,128,128]{2,1,0:T(8,128)(2,1)} %get-tuple-element.551, s32[1024]{0:T(1024)S(1)} %pad_clamp_fusion.8), kind=kCustom, calls=%fused_computation.1.clone.clone.1.clone | custom fusion | bytes 2359440 | tf_op jit(solution)/shard_map/while/body/eval_jaxpr/gather | solution.py:28
  343.4 4.1 %gather_fusion.1 = bf16[36,128,128]{2,1,0:T(8,128)(2,1)S(1)} fusion(bf16[252,128,128]{2,1,0:T(8,128)(2,1)} %get-tuple-element.551, s32[1024]{0:T(1024)S(1)} %pad_clamp_fusion.8), kind=kCustom, calls=%fused_computation.1.clone.clone.1.clone | custom fusion | bytes 2359440 | tf_op jit(solution)/shard_map/while/body/eval_jaxpr/gather | solution.py:28
  349.3 4.1 %gather_fusion.1 = bf16[36,128,128]{2,1,0:T(8,128)(2,1)S(1)} fusion(bf16[252,128,128]{2,1,0:T(8,128)(2,1)} %get-tuple-element.551, s32[1024]{0:T(1024)S(1)} %pad_clamp_fusion.8), kind=kCustom, calls=%fused_computation.1.clone.clone.1.clone | custom fusion | bytes 2359440 | tf_op jit(solution)/shard_map/while/body/eval_jaxpr/gather | solution.py:28
  355.1 4.1 %gather_fusion.1 = bf16[36,128,128]{2,1,0:T(8,128)(2,1)S(1)} fusion(bf16[252,128,128]{2,1,0:T(8,128)(2,1)} %get-tuple-element.551, s32[1024]{0:T(1024)S(1)} %pad_clamp_fusion.8), kind=kCustom, calls=%fused_computation.1.clone.clone.1.clone | custom fusion | bytes 2359440 | tf_op jit(solution)/shard_map/while/body/eval_jaxpr/gather | solution.py:28
  360.5 3.1 subtract_convert_fusion
  (196 shorter events, 57.0 us)
Async XLA Ops:
  0.0 154.3 %copy-start.3 = (s32[3,12]{1,0:T(4,128)S(1)}, s32[3,12]{1,0:T(4,128)}, u32[]{:S(2)}) copy-start(s32[3,12]{1,0:T(4,128)} %param.7) | copy-start | bytes 436
  0.0 150.4 %collective-permute-start.6 = (bf16[3,12,128,128]{3,2,1,0:T(8,128)(2,1)}, bf16[3,12,128,128]{3,2,1,0:T(8,128)(2,1)S(1)}, u32[]{:S(2)}, u32[]{:S(2)}) collective-permute-start(bf16[3,12,128,128]{3,2,1,0:T(8,128)(2,1)} %param.6), channel_id=1, source_target_pairs={{0,3},{1,4},{2,5},{3,6},{4,7},{5,8},{6,9},{7,10},{8,11},{9,12},{10... | collective-permute-start | bytes 3538952 | tf_op jit(solution)/shard_map/ppermute | solution.py:12
  5.7 150.8 %collective-permute-start.7 = (bf16[3,12,128,128]{3,2,1,0:T(8,128)(2,1)}, bf16[3,12,128,128]{3,2,1,0:T(8,128)(2,1)}, u32[]{:S(2)}, u32[]{:S(2)}) collective-permute-start(bf16[3,12,128,128]{3,2,1,0:T(8,128)(2,1)} %param.6), channel_id=1, source_target_pairs={{0,2},{1,3},{2,4},{3,5},{4,6},{5,7},{6,8},{7,9},{8,10},{9,11},{10,... | collective-permute-start | bytes 3538952 | tf_op jit(solution)/shard_map/ppermute | solution.py:12
  9.0 149.0 %collective-permute-start.8 = (bf16[3,12,128,128]{3,2,1,0:T(8,128)(2,1)}, bf16[3,12,128,128]{3,2,1,0:T(8,128)(2,1)}, u32[]{:S(2)}, u32[]{:S(2)}) collective-permute-start(bf16[3,12,128,128]{3,2,1,0:T(8,128)(2,1)} %param.6), channel_id=1, source_target_pairs={{0,1},{1,2},{2,3},{3,4},{4,5},{5,6},{6,7},{7,8},{8,9},{9,10},{10,1... | collective-permute-start | bytes 3538952 | tf_op jit(solution)/shard_map/ppermute | solution.py:12
  11.2 148.7 %collective-permute-start.9 = (bf16[3,12,128,128]{3,2,1,0:T(8,128)(2,1)}, bf16[3,12,128,128]{3,2,1,0:T(8,128)(2,1)S(1)}, u32[]{:S(2)}, u32[]{:S(2)}) collective-permute-start(bf16[3,12,128,128]{3,2,1,0:T(8,128)(2,1)} %param.6), channel_id=1, source_target_pairs={{0,511},{1,0},{2,1},{3,2},{4,3},{5,4},{6,5},{7,6},{8,7},{9,8},{10,... | collective-permute-start | bytes 3538952 | tf_op jit(solution)/shard_map/ppermute | solution.py:12
  14.7 67.7 %collective-permute-start = (s32[3,12]{1,0:T(4,128)}, s32[3,12]{1,0:T(4,128)S(1)}, u32[]{:S(2)}, u32[]{:S(2)}) collective-permute-start(s32[3,12]{1,0:T(4,128)} %param.7), channel_id=1, source_target_pairs={{0,3},{1,4},{2,5},{3,6},{4,7},{5,8},{6,9},{7,10},{8,11},{9,12},{10... | collective-permute-start | bytes 440 | tf_op jit(solution)/shard_map/ppermute | solution.py:12
  82.5 14.0 %collective-permute-start.1 = (s32[3,12]{1,0:T(4,128)}, s32[3,12]{1,0:T(4,128)S(1)}, u32[]{:S(2)}, u32[]{:S(2)}) collective-permute-start(s32[3,12]{1,0:T(4,128)} %param.7), channel_id=1, source_target_pairs={{0,2},{1,3},{2,4},{3,5},{4,6},{5,7},{6,8},{7,9},{8,10},{9,11},{10,... | collective-permute-start | bytes 440 | tf_op jit(solution)/shard_map/ppermute | solution.py:12
  96.5 12.6 %collective-permute-start.2 = (s32[3,12]{1,0:T(4,128)}, s32[3,12]{1,0:T(4,128)S(1)}, u32[]{:S(2)}, u32[]{:S(2)}) collective-permute-start(s32[3,12]{1,0:T(4,128)} %param.7), channel_id=1, source_target_pairs={{0,1},{1,2},{2,3},{3,4},{4,5},{5,6},{6,7},{7,8},{8,9},{9,10},{10,1... | collective-permute-start | bytes 440 | tf_op jit(solution)/shard_map/ppermute | solution.py:12
  109.1 10.7 %collective-permute-start.3 = (s32[3,12]{1,0:T(4,128)}, s32[3,12]{1,0:T(4,128)S(1)}, u32[]{:S(2)}, u32[]{:S(2)}) collective-permute-start(s32[3,12]{1,0:T(4,128)} %param.7), channel_id=1, source_target_pairs={{0,511},{1,0},{2,1},{3,2},{4,3},{5,4},{6,5},{7,6},{8,7},{9,8},{10,... | collective-permute-start | bytes 440 | tf_op jit(solution)/shard_map/ppermute | solution.py:12
  119.8 10.1 %collective-permute-start.4 = (s32[3,12]{1,0:T(4,128)}, s32[3,12]{1,0:T(4,128)S(1)}, u32[]{:S(2)}, u32[]{:S(2)}) collective-permute-start(s32[3,12]{1,0:T(4,128)} %param.7), channel_id=1, source_target_pairs={{0,510},{1,511},{2,0},{3,1},{4,2},{5,3},{6,4},{7,5},{8,6},{9,7},{1... | collective-permute-start | bytes 440 | tf_op jit(solution)/shard_map/ppermute | solution.py:12
  129.9 6.1 %collective-permute-start.5 = (s32[3,12]{1,0:T(4,128)}, s32[3,12]{1,0:T(4,128)S(1)}, u32[]{:S(2)}, u32[]{:S(2)}) collective-permute-start(s32[3,12]{1,0:T(4,128)} %param.7), channel_id=1, source_target_pairs={{0,509},{1,510},{2,511},{3,0},{4,1},{5,2},{6,3},{7,4},{8,5},{9,6},... | collective-permute-start | bytes 440 | tf_op jit(solution)/shard_map/ppermute | solution.py:12
  136.0 43.8 %collective-permute-start.10 = (bf16[3,12,128,128]{3,2,1,0:T(8,128)(2,1)}, bf16[3,12,128,128]{3,2,1,0:T(8,128)(2,1)}, u32[]{:S(2)}, u32[]{:S(2)}) collective-permute-start(bf16[3,12,128,128]{3,2,1,0:T(8,128)(2,1)} %param.6), channel_id=1, source_target_pairs={{0,510},{1,511},{2,0},{3,1},{4,2},{5,3},{6,4},{7,5},{8,6},{9,7},{1... | collective-permute-start | bytes 3538952 | tf_op jit(solution)/shard_map/ppermute | solution.py:12
  150.4 3.6 copy-start.2
  150.5 57.6 %collective-permute-start.11 = (bf16[3,12,128,128]{3,2,1,0:T(8,128)(2,1)}, bf16[3,12,128,128]{3,2,1,0:T(8,128)(2,1)}, u32[]{:S(2)}, u32[]{:S(2)}) collective-permute-start(bf16[3,12,128,128]{3,2,1,0:T(8,128)(2,1)} %param.6), channel_id=1, source_target_pairs={{0,509},{1,510},{2,511},{3,0},{4,1},{5,2},{6,3},{7,4},{8,5},{9,6},... | collective-permute-start | bytes 3538952 | tf_op jit(solution)/shard_map/ppermute | solution.py:12
  158.0 1.6 copy-start.1
  209.6 3.2 copy-start
where the time goes:
time: 366 us; the launch traced here: 364 us
  waiting for transfers between devices  133 us (36%)
  local copies, waits for them, and re-layouts  114 us (31%)
  starting transfers between devices  66.1 us (18%)
  matrix products  36.8 us (10%)
  other arithmetic  13.4 us (4%)
    ppermute x12, waiting for transfers between devices, passed_along(): return lax.ppermute(value, axis, pairs)  133 us
    gather x24, local copies, waits for them, and re-layouts, one_slot(): selected = flattened[near_index * slot_count + position]  98.9 us
    ppermute x12, starting transfers between devices, passed_along(): return lax.ppermute(value, axis, pairs)  66.1 us
    dot_general x24, matrix products, one_slot(): jnp.einsum('cknm,ckmq->cnq', selected, right, preferred_element_type=jnp....  36.8 us
    unnamed x15, local copies, waits for them, and re-layouts  10.2 us
  transfers between devices with their start and end apart: 12, of which 8 were waited for; matrix products, arithmetic and copies ran while one was open for 2% of the time, Pallas kernels for 0%

commit v1 on v0

v1 whole, which is shorter than its diff:
```python
import jax
import jax.numpy as jnp
from jax import lax
from jax.experimental import pallas as pl
from jax.experimental.pallas import tpu as pltpu
from jax.sharding import PartitionSpec as P

AXES = ("row", "col", "layer")
BAND = 8
TILE = 128
SLOTS = 12
COLS = 3
OWN = COLS * SLOTS
META = 16
BODY = OWN * TILE
FULL = META + BODY + META
FAR = BAND + 1
NEAR = BAND + 2
RELAY = FAR + NEAR
SHARED = 6 * OWN
ZERO = SHARED + RELAY
BLOCKS = ZERO + 1
WIDE = SLOTS * TILE
ANY = pl.BlockSpec(memory_space=pl.ANY)


def send(value, pairs):
    return lax.ppermute(value, AXES, pairs)


def pack_kernel(blocks, meta, out, sem):
    copies = [
        pltpu.make_async_copy(meta, out.at[pl.ds(0, META)], sem.at[0]),
        pltpu.make_async_copy(meta, out.at[pl.ds(META + BODY, META)], sem.at[1]),
    ]
    for c in range(COLS):
        copies.append(
            pltpu.make_async_copy(
                blocks.at[pl.ds(c * WIDE, WIDE)],
                out.at[pl.ds(META + c * WIDE, WIDE)],
                sem.at[2 + c],
            )
        )
    for copy in copies:
        copy.start()
    for copy in copies:
        copy.wait()


def pack(blocks, meta):
    return pl.pallas_call(
        pack_kernel,
        out_shape=jax.ShapeDtypeStruct((FULL, TILE), jnp.bfloat16),
        in_specs=[ANY, ANY],
        out_specs=ANY,
        scratch_shapes=[pltpu.SemaphoreType.DMA((2 + COLS,))],
        cost_estimate=pl.CostEstimate(flops=0, bytes_accessed=4 * BODY * TILE, transcendentals=0),
    )(blocks, meta)


def relay_kernel(index, packed, out, zeros, sem):
    zeros[...] = jnp.zeros_like(zeros)

    def start(i, carry):
        where = index[i]
        target = out.at[pl.ds(pl.multiple_of(i * TILE, TILE), TILE)]

        @pl.when(where < OWN)
        def _():
            source = pl.multiple_of(META + where * TILE, META)
            pltpu.make_async_copy(packed.at[pl.ds(source, TILE)], target, sem).start()

        @pl.when(where >= OWN)
        def _():
            pltpu.make_async_copy(zeros, target, sem).start()

        return carry

    lax.fori_loop(0, RELAY, start, 0)
    pltpu.make_async_copy(out, out, sem).wait()


def relay_blocks(index, packed):
    return pl.pallas_call(
        relay_kernel,
        out_shape=jax.ShapeDtypeStruct((RELAY * TILE, TILE), jnp.bfloat16),
        in_specs=[pl.BlockSpec(memory_space=pltpu.SMEM), ANY],
        out_specs=ANY,
        scratch_shapes=[pltpu.VMEM((TILE, TILE), jnp.bfloat16), pltpu.SemaphoreType.DMA],
        cost_estimate=pl.CostEstimate(
            flops=0, bytes_accessed=4 * RELAY * TILE * TILE, transcendentals=0
        ),
    )(index, packed)


def refine_kernel(index, own, f, g, x0, xf, xg, relay, out, near, left, square, sem):
    copies = [pltpu.make_async_copy(own, near.at[pl.ds(0, BODY)], sem.at[0])]
    for i, packed in enumerate((f, g, x0, xf, xg), 1):
        copies.append(
            pltpu.make_async_copy(
                packed.at[pl.ds(META, BODY)], near.at[pl.ds(i * BODY, BODY)], sem.at[i]
            )
        )
    copies.append(
        pltpu.make_async_copy(
            relay, near.at[pl.ds(SHARED * TILE, RELAY * TILE)], sem.at[6]
        )
    )
    for copy in copies:
        copy.start()
    near[pl.ds(ZERO * TILE, TILE), :] = jnp.zeros((TILE, TILE), jnp.bfloat16)
    for copy in copies:
        copy.wait()
    for c in range(COLS):

        def gather(s, carry):
            for k in range(SLOTS):
                where = index[(c * SLOTS + s) * SLOTS + k]
                left[pl.ds(pl.multiple_of(s * TILE, TILE), TILE), pl.ds(k * TILE, TILE)] = near[
                    pl.ds(pl.multiple_of(where * TILE, TILE), TILE), :
                ]
            return carry

        lax.fori_loop(0, SLOTS, gather, 0)
        square[...] = jnp.dot(
            left[...], near[pl.ds(c * WIDE, WIDE), :], preferred_element_type=jnp.float32
        ).astype(jnp.bfloat16)
        cubed = jnp.dot(left[...], square[...], preferred_element_type=jnp.float32)
        out[pl.ds(c * WIDE, WIDE), :] = (
            3.0 * square[...].astype(jnp.float32) - 2.0 * cubed
        ).astype(jnp.bfloat16)


def refine(index, own, *parts):
    return pl.pallas_call(
        refine_kernel,
        out_shape=jax.ShapeDtypeStruct((BODY, TILE), jnp.bfloat16),
        in_specs=[pl.BlockSpec(memory_space=pltpu.SMEM)] + [ANY] * 7,
        out_specs=pl.BlockSpec(memory_space=pltpu.VMEM),
        scratch_shapes=[
            pltpu.VMEM((BLOCKS * TILE, TILE), jnp.bfloat16),
            pltpu.VMEM((WIDE, WIDE), jnp.bfloat16),
            pltpu.VMEM((WIDE, TILE), jnp.bfloat16),
            pltpu.SemaphoreType.DMA((7,)),
        ],
        compiler_params=pltpu.CompilerParams(vmem_limit_bytes=40 * 2**20),
        cost_estimate=pl.CostEstimate(
            flops=4 * COLS * WIDE * WIDE * TILE, bytes_accessed=2 * BLOCKS * TILE * TILE, transcendentals=0
        ),
    )(index, own, *parts)


def shards(blocks, block_rows):
    count = lax.axis_size(AXES)
    device = lax.axis_index(AXES)
    odd = device % 2
    total = COLS * count
    columns = device * COLS + jnp.arange(COLS, dtype=jnp.int32)
    offsets = (block_rows - columns[:, None] + total // 2) % total - total // 2
    meta = jnp.zeros((META, TILE), jnp.bfloat16).at[:COLS, :SLOTS].set(offsets.astype(jnp.bfloat16))
    own = blocks.reshape(BODY, TILE)
    packed = pack(own, meta)

    devices = range(count)
    outward = [(s, (s + (2 if s % 2 else -2)) % count) for s in devices]
    inward = [(s, (s + (-2 if s % 2 else 2)) % count) for s in devices]
    across = [(s, s ^ 1) for s in devices]
    onward = [(s, (s + (1 if s % 2 else -1)) % count) for s in devices]

    def read_meta(part):
        return part[:COLS, :SLOTS].astype(jnp.int32)

    f = send(packed, outward)
    x0 = send(packed, across)
    g = send(packed, inward)

    far = jnp.arange(FAR, dtype=jnp.int32)
    near = jnp.arange(NEAR, dtype=jnp.int32)
    away = jnp.concatenate([far, near - 1])
    here = jnp.concatenate([far - BAND, near - BAND])
    relay_wanted = jnp.where(odd == 1, away, here)
    relay_column = jnp.where(jnp.arange(RELAY) < FAR, 1, 2 * odd)
    f_meta = read_meta(f)
    f_keys = (f_meta + jnp.arange(COLS, dtype=jnp.int32)[:, None] * 64).reshape(1, OWN)
    hits = (relay_wanted + relay_column * 64)[:, None] == f_keys
    relay_index = jnp.min(
        jnp.where(hits, jnp.arange(OWN, dtype=jnp.int32)[None, :], OWN), axis=1
    )
    relay = send(relay_blocks(relay_index, f), onward)
    xf = send(f, across)
    xg = send(g, across)

    side = 1 - 2 * odd
    local = jnp.arange(COLS, dtype=jnp.int32)[:, None]

    def keys(first, meta):
        column = first + local
        return ((column + meta + 32) * 64 + column + 32).reshape(1, OWN)

    relay_column = jnp.where(
        odd == 1,
        jnp.where(jnp.arange(RELAY) < FAR, 10, 9),
        jnp.where(jnp.arange(RELAY) < FAR, -8, -7),
    )
    relay_offset = jnp.where(odd == 1, here, away)
    all_keys = jnp.concatenate(
        [
            keys(0, offsets),
            keys(6 * side, f_meta),
            keys(-6 * side, read_meta(g)),
            keys(3 * side, read_meta(x0)),
            keys(-3 * side, read_meta(xf)),
            keys(9 * side, read_meta(xg)),
            ((relay_column + relay_offset + 32) * 64 + relay_column + 32).reshape(1, RELAY),
        ],
        axis=1,
    )
    places = local + offsets
    wanted = ((places[:, :, None] + 32) * 64 + places[:, None, :] + 32).reshape(-1, 1)
    index = jnp.min(
        jnp.where(wanted == all_keys, jnp.arange(ZERO, dtype=jnp.int32)[None, :], ZERO), axis=1
    )
    result = refine(index, own, f, g, x0, xf, xg, relay)
    return result.reshape(COLS, SLOTS, TILE, TILE)


def solution(mesh):
    placed = (P(AXES, None, None, None), P(AXES, None))
    return jax.shard_map(
        shards,
        mesh=mesh,
        in_specs=placed,
        out_specs=P(AXES, None, None, None),
        check_vma=False,
    )
```

time: 366 us -> 143 us (0.39)
  the two profiles are of different devices: /device:TPU:1 before, /device:TPU:0 now
where the time goes in v1:
time: 143 us; the launch traced here: 142 us
  Pallas kernels  75 us (52%)
  starting transfers between devices  31.8 us (22%)
  other arithmetic  14.1 us (10%)
  local copies, waits for them, and re-layouts  11.8 us (8%)
  waiting for transfers between devices  9.55 us (7%)
    pallas_call x1, Pallas kernels, pack(): pl.pallas_call(pack_kernel, out_shape=jax.ShapeDtypeStruct((FULL, TILE),...  37.1 us
    ppermute x6, starting transfers between devices, send(): return lax.ppermute(value, AXES, pairs)  31.8 us
    pallas_call x1, Pallas kernels, refine(): pl.pallas_call(refine_kernel, out_shape=jax.ShapeDtypeStruct((BODY, TILE)...  22.2 us
    pallas_call x1, Pallas kernels, relay_blocks(): pl.pallas_call(relay_kernel, out_shape=jax.ShapeDtypeStruct((RELAY * TILE...  15.7 us
    ppermute x6, waiting for transfers between devices, send(): return lax.ppermute(value, AXES, pairs)  9.55 us
    reshape x6, local copies, waits for them, and re-layouts, keys(): return ((column + meta + 32) * 64 + column + 32).reshape(1, OWN)  6.48 us
    add x4, other arithmetic, keys(): return ((column + meta + 32) * 64 + column + 32).reshape(1, OWN)  4.58 us
  transfers between devices with their start and end apart: 6, of which 2 were waited for; matrix products, arithmetic and copies ran while one was open for 16% of the time, Pallas kernels for 11%

profile of v1, /device:TPU:0, one launch (start us, length us, event | category | flops | bytes accessed | tf_op | source)
XLA Modules:
  0.0 142.4 jit_solution(13938624382596161169)
XLA Ops:
  0.0 1.4 add_multiply_fusion
  1.4 0.6 iota_add_fusion
  1.9 0.6 scatter.4.meta
  2.5 37.1 %shard_map.28 = bf16[4640,128]{1,0:T(8,128)(2,1)} custom-call(bf16[4608,128]{1,0:T(8,128)(2,1)} %bitcast.9, bf16[16,128]{1,0:T(8,128)(2,1)} %scatter.4.meta), custom_call_target="tpu_custom_call" | custom-call | bytes 2359296 | tf_op jit(solution)/shard_map/pallas_call | solution.py:51
  39.7 0.0 copy-start.2
  39.7 2.1 %collective-permute-start.1 = (bf16[4640,128]{1,0:T(8,128)(2,1)}, bf16[4640,128]{1,0:T(8,128)(2,1)S(1)}, u32[]{:S(2)}, u32[]{:S(2)}) collective-permute-start(bf16[4640,128]{1,0:T(8,128)(2,1)} %shard_map.28), channel_id=1, source_target_pairs={{0,2},{1,511},{2,4},{3,1},{4,6},{5,3},{6,8},{7,5},{8,10},{9,7},{10... | collective-permute-start | bytes 3563528 | tf_op jit(solution)/shard_map/ppermute | solution.py:28
  41.8 10.2 %collective-permute-start.2 = (bf16[4640,128]{1,0:T(8,128)(2,1)}, bf16[4640,128]{1,0:T(8,128)(2,1)}, u32[]{:S(2)}, u32[]{:S(2)}) collective-permute-start(bf16[4640,128]{1,0:T(8,128)(2,1)} %shard_map.28), channel_id=1, source_target_pairs={{0,1},{1,0},{2,3},{3,2},{4,5},{5,4},{6,7},{7,6},{8,9},{9,8},{10,11... | collective-permute-start | bytes 3563528 | tf_op jit(solution)/shard_map/ppermute | solution.py:28
  52.0 3.3 %collective-permute-start = (bf16[4640,128]{1,0:T(8,128)(2,1)}, bf16[4640,128]{1,0:T(8,128)(2,1)S(1)}, u32[]{:S(2)}, u32[]{:S(2)}) collective-permute-start(bf16[4640,128]{1,0:T(8,128)(2,1)} %shard_map.28), channel_id=1, source_target_pairs={{0,510},{1,3},{2,0},{3,5},{4,2},{5,7},{6,4},{7,9},{8,6},{9,11},{10... | collective-permute-start | bytes 3563528 | tf_op jit(solution)/shard_map/ppermute | solution.py:28
  55.3 1.3 reshape.215
  56.6 1.4 add_add_fusion
  58.0 1.4 add.348
  59.4 0.5 iota_add_fusion.7
  59.9 0.5 iota_add_fusion.6
  60.4 0.5 iota_add_fusion.5
  60.9 0.5 iota_add_fusion.4
  61.5 6.3 %collective-permute-done.1.g = bf16[4640,128]{1,0:T(8,128)(2,1)S(1)} collective-permute-done((bf16[4640,128]{1,0:T(8,128)(2,1)}, bf16[4640,128]{1,0:T(8,128)(2,1)S(1)}, u32[]{:S(2)}, u32[]{:S(2)}) %collective-permute-start.1) | collective-permute-done | bytes 1187872 | tf_op jit(solution)/shard_map/ppermute | solution.py:28
  67.8 4.5 %collective-permute-start.4 = (bf16[4640,128]{1,0:T(8,128)(2,1)S(1)}, bf16[4640,128]{1,0:T(8,128)(2,1)}, u32[]{:S(2)}, u32[]{:S(2)}) collective-permute-start(bf16[4640,128]{1,0:T(8,128)(2,1)S(1)} %collective-permute-done.1.g), channel_id=1, source_target_pairs={{0,1},{1,0},{2,3},{3,2},{4,5},{5,4},{6,7},{7,6},{8,9},{9,8},{10,11... | collective-permute-start | bytes 3563528 | tf_op jit(solution)/shard_map/ppermute | solution.py:28
  72.3 0.7 add_add_fusion.6
  73.0 3.2 %collective-permute-done.packed.f = bf16[4640,128]{1,0:T(8,128)(2,1)S(1)} collective-permute-done((bf16[4640,128]{1,0:T(8,128)(2,1)}, bf16[4640,128]{1,0:T(8,128)(2,1)S(1)}, u32[]{:S(2)}, u32[]{:S(2)}) %collective-permute-start) | collective-permute-done | bytes 1187872 | tf_op jit(solution)/shard_map/ppermute | solution.py:28
  76.2 0.0 copy-start
  76.2 3.2 %collective-permute-start.3 = (bf16[4640,128]{1,0:T(8,128)(2,1)S(1)}, bf16[4640,128]{1,0:T(8,128)(2,1)}, u32[]{:S(2)}, u32[]{:S(2)}) collective-permute-start(bf16[4640,128]{1,0:T(8,128)(2,1)S(1)} %collective-permute-done.packed.f), channel_id=1, source_target_pairs={{0,1},{1,0},{2,3},{3,2},{4,5},{5,4},{6,7},{7,6},{8,9},{9,8},{10,11... | collective-permute-start | bytes 3563528 | tf_op jit(solution)/shard_map/ppermute | solution.py:28
  79.4 0.6 fusion.7
  80.0 0.7 convert_add_fusion
  80.7 1.3 eq.45
  82.0 1.3 select_reduce_fusion.1.index
  83.3 0.0 copy-done
  83.3 15.7 %shard_map.29 = bf16[2432,128]{1,0:T(8,128)(2,1)} custom-call(s32[19]{0:T(128)} %select_reduce_fusion.1.index, bf16[4640,128]{1,0:T(8,128)(2,1)} %copy-done), custom_call_target="tpu_custom_call" | custom-call | bytes 1245184 | tf_op jit(solution)/shard_map/pallas_call | solution.py:84
  99.0 8.5 %collective-permute-start.5 = (bf16[2432,128]{1,0:T(8,128)(2,1)}, bf16[2432,128]{1,0:T(8,128)(2,1)}, u32[]{:S(2)}, u32[]{:S(2)}) collective-permute-start(bf16[2432,128]{1,0:T(8,128)(2,1)} %shard_map.29), channel_id=1, source_target_pairs={{0,511},{1,2},{2,1},{3,4},{4,3},{5,6},{6,5},{7,8},{8,7},{9,10},{10... | collective-permute-start | bytes 1867784 | tf_op jit(solution)/shard_map/ppermute | solution.py:28
  107.5 1.3 add_add_fusion.4
  108.7 0.0 collective-permute-done.2.x0
  108.7 1.3 add_add_fusion.3
  110.0 1.3 reshape.219
  111.3 1.3 reshape.218
  112.6 1.2 reshape.217
  113.8 0.0 collective-permute-done.4.xg
  113.8 1.3 add_add_fusion.1
  115.1 1.3 reshape.221
  116.4 0.0 collective-permute-done.3.xf
  116.4 0.8 add_add_fusion.2
  117.1 0.1 reshape.220
  117.2 0.8 concatenate.48
  118.0 0.9 select_reduce_fusion.index
  118.9 0.0 collective-permute-done.5.relay
  118.9 0.0 copy-done.2
  118.9 0.0 copy-start.1
  118.9 1.3 copy-done.1
  120.2 22.2 %shard_map.30 = bf16[4608,128]{1,0:T(8,128)(2,1)} custom-call(s32[432]{0:T(512)S(1)} %select_reduce_fusion.index, bf16[4608,128]{1,0:T(8,128)(2,1)S(1)} %bitcast.10, bf16[4640,128]{1,0:T(8,128)(2,1)S(1)} %copy-done.1, bf16[4640,128]{1,0:T(8,128)(2,1)S(1)} %collective-permute-done.1.g, bf16[4640,128]{1,0:T(8,128)(2,1)} %collective-permute-done.2.x0, ...), custom_call_target="tpu_custom_call" | custom-call | flops 3623878656 | bytes 7733248 | tf_op jit(solution)/shard_map/pallas_call | solution.py:135
  (8 shorter events, 0.0 us)
Async XLA Ops:
  39.7 79.2 %copy-start.2 = (bf16[3,12,128,128]{3,2,1,0:T(8,128)(2,1)S(1)}, bf16[3,12,128,128]{3,2,1,0:T(8,128)(2,1)}, u32[]{:S(2)}) copy-start(bf16[3,12,128,128]{3,2,1,0:T(8,128)(2,1)} %param.4) | copy-start | bytes 3538948
  39.7 28.1 %collective-permute-start.1 = (bf16[4640,128]{1,0:T(8,128)(2,1)}, bf16[4640,128]{1,0:T(8,128)(2,1)S(1)}, u32[]{:S(2)}, u32[]{:S(2)}) collective-permute-start(bf16[4640,128]{1,0:T(8,128)(2,1)} %shard_map.28), channel_id=1, source_target_pairs={{0,2},{1,511},{2,4},{3,1},{4,6},{5,3},{6,8},{7,5},{8,10},{9,7},{10... | collective-permute-start | bytes 3563528 | tf_op jit(solution)/shard_map/ppermute | solution.py:28
  41.8 67.0 %collective-permute-start.2 = (bf16[4640,128]{1,0:T(8,128)(2,1)}, bf16[4640,128]{1,0:T(8,128)(2,1)}, u32[]{:S(2)}, u32[]{:S(2)}) collective-permute-start(bf16[4640,128]{1,0:T(8,128)(2,1)} %shard_map.28), channel_id=1, source_target_pairs={{0,1},{1,0},{2,3},{3,2},{4,5},{5,4},{6,7},{7,6},{8,9},{9,8},{10,11... | collective-permute-start | bytes 3563528 | tf_op jit(solution)/shard_map/ppermute | solution.py:28
  52.0 24.2 %collective-permute-start = (bf16[4640,128]{1,0:T(8,128)(2,1)}, bf16[4640,128]{1,0:T(8,128)(2,1)S(1)}, u32[]{:S(2)}, u32[]{:S(2)}) collective-permute-start(bf16[4640,128]{1,0:T(8,128)(2,1)} %shard_map.28), channel_id=1, source_target_pairs={{0,510},{1,3},{2,0},{3,5},{4,2},{5,7},{6,4},{7,9},{8,6},{9,11},{10... | collective-permute-start | bytes 3563528 | tf_op jit(solution)/shard_map/ppermute | solution.py:28
  67.8 46.1 %collective-permute-start.4 = (bf16[4640,128]{1,0:T(8,128)(2,1)S(1)}, bf16[4640,128]{1,0:T(8,128)(2,1)}, u32[]{:S(2)}, u32[]{:S(2)}) collective-permute-start(bf16[4640,128]{1,0:T(8,128)(2,1)S(1)} %collective-permute-done.1.g), channel_id=1, source_target_pairs={{0,1},{1,0},{2,3},{3,2},{4,5},{5,4},{6,7},{7,6},{8,9},{9,8},{10,11... | collective-permute-start | bytes 3563528 | tf_op jit(solution)/shard_map/ppermute | solution.py:28
  76.2 7.1 %copy-start = (bf16[4640,128]{1,0:T(8,128)(2,1)}, bf16[4640,128]{1,0:T(8,128)(2,1)S(1)}, u32[]{:S(2)}) copy-start(bf16[4640,128]{1,0:T(8,128)(2,1)S(1)} %collective-permute-done.packed.f) | copy-start | bytes 3563524
  76.2 40.2 %collective-permute-start.3 = (bf16[4640,128]{1,0:T(8,128)(2,1)S(1)}, bf16[4640,128]{1,0:T(8,128)(2,1)}, u32[]{:S(2)}, u32[]{:S(2)}) collective-permute-start(bf16[4640,128]{1,0:T(8,128)(2,1)S(1)} %collective-permute-done.packed.f), channel_id=1, source_target_pairs={{0,1},{1,0},{2,3},{3,2},{4,5},{5,4},{6,7},{7,6},{8,9},{9,8},{10,11... | collective-permute-start | bytes 3563528 | tf_op jit(solution)/shard_map/ppermute | solution.py:28
  99.0 19.9 %collective-permute-start.5 = (bf16[2432,128]{1,0:T(8,128)(2,1)}, bf16[2432,128]{1,0:T(8,128)(2,1)}, u32[]{:S(2)}, u32[]{:S(2)}) collective-permute-start(bf16[2432,128]{1,0:T(8,128)(2,1)} %shard_map.29), channel_id=1, source_target_pairs={{0,511},{1,2},{2,1},{3,4},{4,3},{5,6},{6,5},{7,8},{8,7},{9,10},{10... | collective-permute-start | bytes 1867784 | tf_op jit(solution)/shard_map/ppermute | solution.py:28
  118.9 1.3 copy-start.1

commit v2 on v0

v2 whole, which is shorter than its diff:
```python
import functools

import jax
import jax.numpy as jnp
from jax import lax
from jax.experimental import pallas as pl
from jax.experimental.pallas import tpu as pltpu
from jax.sharding import PartitionSpec as P

AXES = ("row", "col", "layer")
BAND = 8
TILE = 128
SLOTS = 12
COLS = 3
OWN = COLS * SLOTS
BODY = OWN * TILE
WIDE = SLOTS * TILE
META = 16
FULL = BODY + META
TALL = WIDE + TILE
FAR = BAND + 1
NEAR = BAND + 2
RELAY = FAR + NEAR
PLACE_AT = 0
ORDER_AT = PLACE_AT + OWN
SLOT_AT = ORDER_AT + OWN
SPAN = 40
SHIFT = 18
FIND_AT = SLOT_AT + OWN
STAGES = 3
TILES_AT = FIND_AT + COLS * SPAN
TABLE = TILES_AT + COLS * STAGES
PAIR = 2 * TILE
PAIRS = SLOTS // 2
CHUNK = 256
BF16 = jnp.bfloat16
F32 = jnp.float32
ANY = pl.BlockSpec(memory_space=pl.ANY)
VMEM = pl.BlockSpec(memory_space=pltpu.VMEM)
SMEM = pl.BlockSpec(memory_space=pltpu.SMEM)


def rows_at(start, size, unit=TILE):
    return pl.ds(pl.multiple_of(start, unit), size)


def call(kernel, out_shape, in_specs, out_specs, scratch, aliases, micros, *args):
    args = [
        pltpu.with_memory_space_constraint(arg, pltpu.VMEM) if spec is VMEM else arg
        for arg, spec in zip(args, in_specs)
    ]
    return pl.pallas_call(
        kernel,
        out_shape=out_shape,
        in_specs=in_specs,
        out_specs=out_specs,
        scratch_shapes=scratch,
        input_output_aliases=aliases,
        compiler_params=pltpu.CompilerParams(vmem_limit_bytes=16 * 2**20),
        cost_estimate=pl.CostEstimate(
            flops=0, bytes_accessed=int(micros * 3e6), transcendentals=0
        ),
    )(*args)


def wrapped(value, total):
    value = jnp.where(value >= total // 2, value - total, value)
    return jnp.where(value < -(total // 2), value + total, value)


def pack_kernel(total, device, rows, mine, packed, wide):
    packed[pl.ds(0, BODY), :] = mine[...]
    column = device[0] * COLS + lax.broadcasted_iota(jnp.int32, (COLS, SLOTS), 0)
    wide[...] = jnp.zeros_like(wide)
    wide[pl.ds(0, COLS), pl.ds(0, SLOTS)] = wrapped(rows[...] - column, total).astype(F32)
    packed[pl.ds(BODY, META), :] = wide[...].astype(BF16)


def table_kernel(total, device, rows, table):
    odd = device[0] % 2
    first = device[0] * COLS
    for c in range(COLS):
        for i in range(SPAN):
            table[FIND_AT + c * SPAN + i] = SLOTS
        places = [wrapped(rows[c, s] - first, total) for s in range(SLOTS)]
        keys, stages = [], []
        for s in range(SLOTS):
            group = (places[s] + BAND + 1) // COLS
            group = jnp.where(odd == 1, 6 - group, group)
            stage = jnp.where(group >= 3, jnp.maximum(group - 4, 0), 3 - group)
            stages.append(stage)
            keys.append(stage * 16 + s)
        for s in range(SLOTS):
            order = jnp.int32(0)
            for other in range(SLOTS):
                if other != s:
                    order = order + jnp.where(keys[other] < keys[s], 1, 0)
            table[PLACE_AT + c * SLOTS + s] = places[s]
            table[ORDER_AT + c * SLOTS + s] = order
            table[SLOT_AT + c * SLOTS + order] = s
            table[FIND_AT + c * SPAN + places[s] + SHIFT] = order
        for stage in range(STAGES):
            held = jnp.int32(0)
            for s in range(SLOTS):
                held = held + jnp.where(stages[s] <= stage, 1, 0)
            table[TILES_AT + c * STAGES + stage] = held // 2


def read_meta(packed, whole, offsets, sem):
    whole[...] = packed[pl.ds(BODY, META), :].astype(F32).astype(jnp.int32)
    copy = pltpu.make_async_copy(whole, offsets, sem)
    copy.start()
    return copy


def scatter(table, left, part, place, offset_at):
    def one(i, carry):
        j = i // COLS
        c = i - j * COLS
        here = FIND_AT + c * SPAN + SHIFT + place + j
        k = table[here]

        @pl.when(k < SLOTS)
        def _():
            for p in range(SLOTS):
                s = table[here + offset_at(j, p)]
                left[
                    rows_at(c * TALL + s * TILE, TILE), rows_at(k * TILE, TILE)
                ] = part[rows_at((j * SLOTS + p) * TILE, TILE), :]

        return carry

    lax.fori_loop(0, COLS * COLS, one, 0)


def accumulate(left, right, total, c, low, high):
    def one(t, carry):
        weights = right[rows_at(c * WIDE + t * PAIR, PAIR), :]
        for m in range(0, WIDE, CHUNK):
            here = rows_at(c * WIDE + m, CHUNK)
            total[here, :] += jnp.dot(
                left[rows_at(c * TALL + m, CHUNK), rows_at(t * PAIR, PAIR, PAIR)],
                weights,
                preferred_element_type=F32,
            )
        return carry

    lax.fori_loop(low, high, one, 0)


def tiles(table, c, stage):
    return table[TILES_AT + c * STAGES + stage]


def finish(table, left, total, c, square, result, out, sem):
    square[...] = total[rows_at(c * WIDE, WIDE), :].astype(BF16)
    for m in range(0, WIDE, CHUNK):
        cubed = jnp.dot(
            left[rows_at(c * TALL + m, CHUNK), :], square[...], preferred_element_type=F32
        )
        refined = (3.0 * square[pl.ds(m, CHUNK), :].astype(F32) - 2.0 * cubed).astype(BF16)
        for i in range(CHUNK // TILE):
            slot = table[SLOT_AT + c * SLOTS + m // TILE + i]
            result[rows_at(slot * TILE, TILE), :] = refined[i * TILE : (i + 1) * TILE]
    copy = pltpu.make_async_copy(result, out.at[rows_at(c * WIDE, WIDE)], sem)
    copy.start()
    return copy


def own_kernel(device, table, mine, x0, left, total, right, whole, offsets, sem):
    side = 1 - 2 * (device[0] % 2)
    copy = read_meta(x0, whole.at[0], offsets.at[0], sem.at[0])

    def clear(i, carry):
        left[rows_at(i * TILE, TILE), :] = jnp.zeros((TILE, WIDE), BF16)
        return carry

    lax.fori_loop(0, COLS * TALL // TILE, clear, 0)
    total[...] = jnp.zeros_like(total)

    def order(i, carry):
        c = i // SLOTS
        right[rows_at(c * WIDE + table[ORDER_AT + i] * TILE, TILE), :] = mine[
            rows_at(i * TILE, TILE), :
        ]
        return carry

    lax.fori_loop(0, OWN, order, 0)
    scatter(table, left, mine, 0, lambda j, p: table[PLACE_AT + j * SLOTS + p] - j)
    copy.wait()
    scatter(table, left, x0, 3 * side, lambda j, p: offsets[0, j, p])
    for c in range(COLS):
        accumulate(left, right, total, c, 0, tiles(table, c, 0))


def outer_kernel(device, table, left_in, total_in, right, f, xf, left, total, whole, offsets, sem):
    del left_in, total_in
    side = 1 - 2 * (device[0] % 2)
    copies = [
        read_meta(part, whole.at[i], offsets.at[i], sem.at[i]) for i, part in enumerate((f, xf))
    ]
    for i, (part, place) in enumerate(((f, 6), (xf, -3))):
        copies[i].wait()
        scatter(table, left, part, place * side, lambda j, p: offsets[i, j, p])
    for c in range(COLS):
        accumulate(left, right, total, c, tiles(table, c, 0), tiles(table, c, 1))


def early_kernel(
    device, table, left_in, total_in, right, g, xg, left, total, out, whole, offsets, square, result, sem
):
    del left_in, total_in
    odd = device[0] % 2
    side = 1 - 2 * odd
    copies = [
        read_meta(part, whole.at[i], offsets.at[i], sem.at[i]) for i, part in enumerate((g, xg))
    ]
    for i, (part, place) in enumerate(((g, -6), (xg, 9))):
        copies[i].wait()
        scatter(table, left, part, place * side, lambda j, p: offsets[i, j, p])
    first = 2 - 2 * odd
    accumulate(left, right, total, first, tiles(table, first, 1), PAIRS)
    copy = finish(table, left, total, first, square, result, out, sem.at[2])
    for c in (1, 2 * odd):
        accumulate(left, right, total, c, tiles(table, c, 1), tiles(table, c, 2))
    copy.wait()


def last_kernel(
    device, table, left_in, total_in, right, relay, out_in, left, total, out, square, result, sem
):
    del left_in, total_in, out_in
    odd = device[0] % 2
    copies = []
    for i, c in enumerate((1, 2 * odd)):
        for start, size, place, low in (
            (0, FAR, jnp.where(odd == 1, 10, -8), jnp.where(odd == 1, -8, 0)),
            (FAR, NEAR, jnp.where(odd == 1, 9, -7), jnp.where(odd == 1, -8, -1)),
        ):
            here = FIND_AT + c * SPAN + SHIFT + place
            k = table[here]

            @pl.when(k < SLOTS)
            def _():
                for p in range(size):
                    s = table[here + low + p]
                    left[
                        rows_at(c * TALL + s * TILE, TILE), rows_at(k * TILE, TILE)
                    ] = relay[pl.ds((start + p) * TILE, TILE), :]

        accumulate(left, right, total, c, tiles(table, c, 2), PAIRS)
        copies.append(finish(table, left, total, c, square, result.at[i], out, sem.at[i]))
    for copy in copies:
        copy.wait()


def relay_kernel(device, f, relay, whole, offsets, sem):
    odd = device[0] % 2
    copy = read_meta(f, whole, offsets, sem)
    relay[...] = jnp.zeros_like(relay)
    copy.wait()
    for column, start, size, shift in (
        (1, 0, FAR, jnp.where(odd == 1, 0, BAND)),
        (2 * odd, FAR, NEAR, jnp.where(odd == 1, 1, BAND)),
    ):

        def one(p, carry):
            at = offsets[column, p] + shift

            @pl.when((at >= 0) & (at < size))
            def _():
                relay[rows_at((start + at) * TILE, TILE), :] = f[
                    rows_at((column * SLOTS + p) * TILE, TILE), :
                ]

            return carry

        lax.fori_loop(0, SLOTS, one, 0)


def send(value, pairs):
    return lax.ppermute(value, AXES, pairs)


def after(*values):
    return lax.optimization_barrier(values)


def meta_scratch(count):
    return [
        pltpu.VMEM((count, META, TILE), jnp.int32),
        pltpu.SMEM((count, META, TILE), jnp.int32),
    ]


def shards(blocks, block_rows):
    count = lax.axis_size(AXES)
    device = lax.axis_index(AXES)
    columns = COLS * count
    devices = range(count)
    outward = [(s, (s + (2 if s % 2 else -2)) % count) for s in devices]
    inward = [(s, (s + (-2 if s % 2 else 2)) % count) for s in devices]
    onward = [(s, (s + (1 if s % 2 else -1)) % count) for s in devices]
    across = [(s, s ^ 1) for s in devices]

    mine = blocks.reshape(BODY, TILE)
    device = device.astype(jnp.int32).reshape(1)
    packed = call(
        functools.partial(pack_kernel, columns),
        pltpu.VMEM((FULL, TILE), BF16),
        [SMEM, VMEM, VMEM],
        VMEM,
        [pltpu.VMEM((META, TILE), F32)],
        {},
        1,
        device,
        block_rows,
        mine,
    )
    f = send(packed, outward)
    x0 = send(packed, across)
    packed, x0 = after(packed, x0)
    g = send(packed, inward)

    table = call(
        functools.partial(table_kernel, columns),
        jax.ShapeDtypeStruct((TABLE,), jnp.int32),
        [SMEM, SMEM],
        SMEM,
        [],
        {},
        2,
        device,
        block_rows,
    )
    left_shape = pltpu.VMEM((COLS * TALL, WIDE), BF16)
    total_shape = pltpu.VMEM((BODY, TILE), F32)
    out_shape = jax.ShapeDtypeStruct((BODY, TILE), BF16)
    left, total, right = call(
        own_kernel,
        (left_shape, total_shape, pltpu.VMEM((BODY, TILE), BF16)),
        [SMEM, SMEM, VMEM, VMEM],
        (VMEM, VMEM, VMEM),
        [*meta_scratch(1), pltpu.SemaphoreType.DMA((1,))],
        {},
        6,
        device,
        table,
        mine,
        x0,
    )

    f, left = after(f, left)
    relay = call(
        relay_kernel,
        pltpu.VMEM((RELAY * TILE, TILE), BF16),
        [SMEM, VMEM],
        VMEM,
        [
            pltpu.VMEM((META, TILE), jnp.int32),
            pltpu.SMEM((META, TILE), jnp.int32),
            pltpu.SemaphoreType.DMA,
        ],
        {},
        1,
        device,
        f,
    )
    f, relay = after(f, relay)
    relay = send(relay, onward)
    xf = send(f, across)
    xg = send(g, across)
    xf, g = after(xf, g)
    left, total = call(
        outer_kernel,
        (left_shape, total_shape),
        [SMEM, SMEM] + [VMEM] * 5,
        (VMEM, VMEM),
        [*meta_scratch(2), pltpu.SemaphoreType.DMA((2,))],
        {2: 0, 3: 1},
        4,
        device,
        table,
        left,
        total,
        right,
        f,
        xf,
    )
    left, total, out = call(
        early_kernel,
        (left_shape, total_shape, out_shape),
        [SMEM, SMEM] + [VMEM] * 5,
        (VMEM, VMEM, ANY),
        [
            *meta_scratch(2),
            pltpu.VMEM((WIDE, TILE), BF16),
            pltpu.VMEM((WIDE, TILE), BF16),
            pltpu.SemaphoreType.DMA((3,)),
        ],
        {2: 0, 3: 1},
        4,
        device,
        table,
        left,
        total,
        right,
        g,
        xg,
    )
    out = call(
        last_kernel,
        (left_shape, total_shape, out_shape),
        [SMEM, SMEM] + [VMEM] * 4 + [ANY],
        (VMEM, VMEM, ANY),
        [
            pltpu.VMEM((WIDE, TILE), BF16),
            pltpu.VMEM((2, WIDE, TILE), BF16),
            pltpu.SemaphoreType.DMA((2,)),
        ],
        {2: 0, 3: 1, 6: 2},
        4,
        device,
        table,
        left,
        total,
        right,
        relay,
        out,
    )[2]
    return out.reshape(COLS, SLOTS, TILE, TILE)


def solution(mesh):
    placed = (P(AXES, None, None, None), P(AXES, None))
    return jax.shard_map(
        shards,
        mesh=mesh,
        in_specs=placed,
        out_specs=P(AXES, None, None, None),
        check_vma=False,
    )
```

time: 366 us -> 70.2 us (0.19)
  waiting for transfers between devices: 133 us -> 6.69 us
  local copies, waits for them, and re-layouts: 114 us -> 1.95 us
  matrix products: 36.8 us -> 0 us
  starting transfers between devices: 66.1 us -> 34.7 us
  Pallas kernels: 0 us -> 26.5 us
  other arithmetic: 13.4 us -> 0 us
    ppermute x12 -> x6, waiting for transfers between devices: 133 us -> 6.69 us  [send(): return lax.ppermute(value, AXES, pairs)]
    gather x26 -> x0, local copies, waits for them, and re-layouts: 99.5 us -> none  [the longest x24 98.9 us: one_slot(): selected = flattened[near_index * slot_count + position]]
    dot_general x24 -> x0, matrix products: 36.8 us -> none  [one_slot(): jnp.einsum('cknm,ckmq->cnq', selected, right, preferred_element_type=jnp....]
    ppermute x12 -> x6, starting transfers between devices: 66.1 us -> 34.7 us  [send(): return lax.ppermute(value, AXES, pairs)]
    pallas_call x0 -> x7, Pallas kernels: none -> 26.5 us  [call(): pl.pallas_call(kernel, out_shape=out_shape, in_specs=in_specs, out_specs=...]
    unnamed x15 -> x6, local copies, waits for them, and re-layouts: 10.2 us -> 1.95 us
    reduce_or x24 -> x0, other arithmetic: 5.16 us -> none  [one_slot(): present = jnp.any(matches, axis=2)]
    reduce_sum x24 -> x0, other arithmetic: 3.69 us -> none  [one_slot(): position = jnp.sum(jnp.where(matches, slot_ids, 0), axis=2)]
  transfers between devices with their start and end apart: 12 -> 6, of which waited for: 8 -> 2; matrix products, arithmetic and copies ran while one was open for 2% -> 0% of each run, Pallas kernels for 0% -> 31%
where the time goes in v2:
time: 70.2 us; the launch traced here: 69.9 us
  starting transfers between devices  34.7 us (49%)
  Pallas kernels  26.5 us (38%)
  waiting for transfers between devices  6.69 us (10%)
  local copies, waits for them, and re-layouts  1.95 us (3%)
    ppermute x6, starting transfers between devices, send(): return lax.ppermute(value, AXES, pairs)  34.7 us
    pallas_call x7, Pallas kernels, call(): pl.pallas_call(kernel, out_shape=out_shape, in_specs=in_specs, out_specs=...  26.5 us
    ppermute x6, waiting for transfers between devices, send(): return lax.ppermute(value, AXES, pairs)  6.69 us
    unnamed x6, local copies, waits for them, and re-layouts  1.95 us
  transfers between devices with their start and end apart: 6, of which 2 were waited for; matrix products, arithmetic and copies ran while one was open for 0% of the time, Pallas kernels for 31%

profile of v2, /device:TPU:1, one launch (start us, length us, event | category | flops | bytes accessed | tf_op | source)
XLA Modules:
  0.0 69.9 jit_solution(5721700768979916039)
XLA Ops:
  0.0 0.0 copy-start
  0.0 1.3 %copy-done = bf16[3,12,128,128]{3,2,1,0:T(8,128)(2,1)S(1)} copy-done((bf16[3,12,128,128]{3,2,1,0:T(8,128)(2,1)S(1)}, bf16[3,12,128,128]{3,2,1,0:T(8,128)(2,1)}, u32[]{:S(2)}) %copy-start) | copy-done | bytes 1179672
  1.3 0.0 copy-start.2
  1.3 0.7 copy-done.2
  2.0 0.0 copy-start.1
  2.0 0.1 shard_map.29
  2.0 8.9 %collective-permute-start.1 = (bf16[4624,128]{1,0:T(8,128)(2,1)S(1)}, bf16[4624,128]{1,0:T(8,128)(2,1)S(1)}, u32[]{:S(2)}, u32[]{:S(2)}) collective-permute-start(bf16[4624,128]{1,0:T(8,128)(2,1)S(1)} %shard_map.29), channel_id=1, source_target_pairs={{0,1},{1,0},{2,3},{3,2},{4,5},{5,4},{6,7},{7,6},{8,9},{9,8},{10,11... | collective-permute-start | bytes 3551240 | tf_op jit(solution)/shard_map/ppermute | solution.py:282
  11.0 1.9 %collective-permute-start = (bf16[4624,128]{1,0:T(8,128)(2,1)S(1)}, bf16[4624,128]{1,0:T(8,128)(2,1)S(1)}, u32[]{:S(2)}, u32[]{:S(2)}) collective-permute-start(bf16[4624,128]{1,0:T(8,128)(2,1)S(1)} %shard_map.29), channel_id=1, source_target_pairs={{0,510},{1,3},{2,0},{3,5},{4,2},{5,7},{6,4},{7,9},{8,6},{9,11},{10... | collective-permute-start | bytes 3551240 | tf_op jit(solution)/shard_map/ppermute | solution.py:282
  12.9 0.5 collective-permute-done.1.x0
  13.4 10.4 %collective-permute-start.3 = (bf16[4624,128]{1,0:T(8,128)(2,1)S(1)}, bf16[4624,128]{1,0:T(8,128)(2,1)S(1)}, u32[]{:S(2)}, u32[]{:S(2)}) collective-permute-start(bf16[4624,128]{1,0:T(8,128)(2,1)S(1)} %shard_map.29), channel_id=1, source_target_pairs={{0,2},{1,511},{2,4},{3,1},{4,6},{5,3},{6,8},{7,5},{8,10},{9,7},{10... | collective-permute-start | bytes 3551240 | tf_op jit(solution)/shard_map/ppermute | solution.py:282
  23.8 2.2 %shard_map.28.table = s32[237]{0:T(256)S(1)} custom-call(s32[1]{0:T(128)} %bitcast.device, s32[3,12]{1,0:T(4,128)S(1)} %copy-done.2), custom_call_target="tpu_custom_call" | custom-call | bytes 6000000 | tf_op jit(solution)/shard_map/pallas_call | solution.py:52
  26.0 0.0 copy-done.1
  26.1 6.1 %shard_map.30 = (bf16[4992,1536]{1,0:T(8,128)(2,1)S(1)}, f32[4608,128]{1,0:T(8,128)S(1)}, bf16[4608,128]{1,0:T(8,128)(2,1)S(1)}) custom-call(s32[1]{0:T(128)} %bitcast.device, s32[237]{0:T(256)S(1)} %shard_map.28.table, bf16[4608,128]{1,0:T(8,128)(2,1)S(1)} %bitcast.4, bf16[4624,128]{1,0:T(8,128)(2,1)S(1)} %collective-permute-done.1.x0), custom_call_target="tpu_custom_call" | custom-call | bytes 18000000 | tf_op jit(solution)/shard_map/pallas_call | solution.py:52
  32.2 6.1 %collective-permute-done.f = bf16[4624,128]{1,0:T(8,128)(2,1)S(1)} collective-permute-done((bf16[4624,128]{1,0:T(8,128)(2,1)S(1)}, bf16[4624,128]{1,0:T(8,128)(2,1)S(1)}, u32[]{:S(2)}, u32[]{:S(2)}) %collective-permute-start) | collective-permute-done | bytes 1183776 | tf_op jit(solution)/shard_map/ppermute | solution.py:282
  38.3 1.2 %shard_map.31 = bf16[2432,128]{1,0:T(8,128)(2,1)S(1)} custom-call(s32[1]{0:T(128)} %bitcast.device, bf16[4624,128]{1,0:T(8,128)(2,1)S(1)} %collective-permute-done.f), custom_call_target="tpu_custom_call" | custom-call | bytes 3000000 | tf_op jit(solution)/shard_map/pallas_call | solution.py:52
  39.5 9.6 %collective-permute-start.2 = (bf16[4624,128]{1,0:T(8,128)(2,1)S(1)}, bf16[4624,128]{1,0:T(8,128)(2,1)S(1)}, u32[]{:S(2)}, u32[]{:S(2)}) collective-permute-start(bf16[4624,128]{1,0:T(8,128)(2,1)S(1)} %collective-permute-done.f), channel_id=1, source_target_pairs={{0,1},{1,0},{2,3},{3,2},{4,5},{5,4},{6,7},{7,6},{8,9},{9,8},{10,11... | collective-permute-start | bytes 3551240 | tf_op jit(solution)/shard_map/ppermute | solution.py:282
  49.2 0.0 collective-permute-done.3.g
  49.2 1.9 %collective-permute-start.4 = (bf16[4624,128]{1,0:T(8,128)(2,1)S(1)}, bf16[4624,128]{1,0:T(8,128)(2,1)S(1)}, u32[]{:S(2)}, u32[]{:S(2)}) collective-permute-start(bf16[4624,128]{1,0:T(8,128)(2,1)S(1)} %collective-permute-done.3.g), channel_id=1, source_target_pairs={{0,1},{1,0},{2,3},{3,2},{4,5},{5,4},{6,7},{7,6},{8,9},{9,8},{10,11... | collective-permute-start | bytes 3551240 | tf_op jit(solution)/shard_map/ppermute | solution.py:282
  51.1 1.9 %collective-permute-start.5 = (bf16[2432,128]{1,0:T(8,128)(2,1)S(1)}, bf16[2432,128]{1,0:T(8,128)(2,1)S(1)}, u32[]{:S(2)}, u32[]{:S(2)}) collective-permute-start(bf16[2432,128]{1,0:T(8,128)(2,1)S(1)} %shard_map.31), channel_id=1, source_target_pairs={{0,511},{1,2},{2,1},{3,4},{4,3},{5,6},{6,5},{7,8},{8,7},{9,10},{10... | collective-permute-start | bytes 1867784 | tf_op jit(solution)/shard_map/ppermute | solution.py:282
  53.0 0.0 collective-permute-done.2.xf
  53.0 6.0 %shard_map.32 = (bf16[4992,1536]{1,0:T(8,128)(2,1)S(1)}, f32[4608,128]{1,0:T(8,128)S(1)}) custom-call(s32[1]{0:T(128)} %bitcast.device, s32[237]{0:T(256)S(1)} %shard_map.28.table, bf16[4992,1536]{1,0:T(8,128)(2,1)S(1)} %get-tuple-element.24.left_in, f32[4608,128]{1,0:T(8,128)S(1)} %get-tuple-element.25.total_in, ...), custom_call_target="tpu_custom_call", output_to_operand_aliasing={{0}: (2, {}), {1}: (3, {})} | custom-call | bytes 12000000 | tf_op jit(solution)/shard_map/pallas_call | solution.py:52
  59.0 0.0 collective-permute-done.4.xg
  59.0 5.8 %shard_map.33 = (bf16[4992,1536]{1,0:T(8,128)(2,1)S(1)}, f32[4608,128]{1,0:T(8,128)S(1)}, bf16[4608,128]{1,0:T(8,128)(2,1)}) custom-call(s32[1]{0:T(128)} %bitcast.device, s32[237]{0:T(256)S(1)} %shard_map.28.table, bf16[4992,1536]{1,0:T(8,128)(2,1)S(1)} %get-tuple-element.31.left_in, ...), custom_call_target="tpu_custom_call", output_to_operand_aliasing={{0}: (2, {}), {1}: (3, {})} | custom-call | bytes 12000000 | tf_op jit(solution)/shard_map/pallas_call | solution.py:52
  64.9 0.0 collective-permute-done.5.relay
  64.9 5.1 %shard_map.34 = (bf16[4992,1536]{1,0:T(8,128)(2,1)S(1)}, f32[4608,128]{1,0:T(8,128)S(1)}, bf16[4608,128]{1,0:T(8,128)(2,1)}) custom-call(s32[1]{0:T(128)} %bitcast.device, s32[237]{0:T(256)S(1)} %shard_map.28.table, bf16[4992,1536]{1,0:T(8,128)(2,1)S(1)} %get-tuple-element.34.left_in, ...), custom_call_target="tpu_custom_call", output_to_operand_aliasing={{0}: (2, {}), {1}: (3, {}), {2}: (6, {})} | custom-call | bytes 12000000 | tf_op jit(solution)/shard_map/pallas_call | solution.py:52
Async XLA Ops:
  0.0 1.3 %copy-start = (bf16[3,12,128,128]{3,2,1,0:T(8,128)(2,1)S(1)}, bf16[3,12,128,128]{3,2,1,0:T(8,128)(2,1)}, u32[]{:S(2)}) copy-start(bf16[3,12,128,128]{3,2,1,0:T(8,128)(2,1)} %param.2) | copy-start | bytes 3538948
  1.3 0.7 copy-start.2
  2.0 24.1 %copy-start.1 = (bf16[3,12,128,128]{3,2,1,0:T(8,128)(2,1)S(1)}, bf16[3,12,128,128]{3,2,1,0:T(8,128)(2,1)}, u32[]{:S(2)}) copy-start(bf16[3,12,128,128]{3,2,1,0:T(8,128)(2,1)} %param.2) | copy-start | bytes 3538948
  2.0 11.4 %collective-permute-start.1 = (bf16[4624,128]{1,0:T(8,128)(2,1)S(1)}, bf16[4624,128]{1,0:T(8,128)(2,1)S(1)}, u32[]{:S(2)}, u32[]{:S(2)}) collective-permute-start(bf16[4624,128]{1,0:T(8,128)(2,1)S(1)} %shard_map.29), channel_id=1, source_target_pairs={{0,1},{1,0},{2,3},{3,2},{4,5},{5,4},{6,7},{7,6},{8,9},{9,8},{10,11... | collective-permute-start | bytes 3551240 | tf_op jit(solution)/shard_map/ppermute | solution.py:282
  11.0 27.4 %collective-permute-start = (bf16[4624,128]{1,0:T(8,128)(2,1)S(1)}, bf16[4624,128]{1,0:T(8,128)(2,1)S(1)}, u32[]{:S(2)}, u32[]{:S(2)}) collective-permute-start(bf16[4624,128]{1,0:T(8,128)(2,1)S(1)} %shard_map.29), channel_id=1, source_target_pairs={{0,510},{1,3},{2,0},{3,5},{4,2},{5,7},{6,4},{7,9},{8,6},{9,11},{10... | collective-permute-start | bytes 3551240 | tf_op jit(solution)/shard_map/ppermute | solution.py:282
  13.4 35.7 %collective-permute-start.3 = (bf16[4624,128]{1,0:T(8,128)(2,1)S(1)}, bf16[4624,128]{1,0:T(8,128)(2,1)S(1)}, u32[]{:S(2)}, u32[]{:S(2)}) collective-permute-start(bf16[4624,128]{1,0:T(8,128)(2,1)S(1)} %shard_map.29), channel_id=1, source_target_pairs={{0,2},{1,511},{2,4},{3,1},{4,6},{5,3},{6,8},{7,5},{8,10},{9,7},{10... | collective-permute-start | bytes 3551240 | tf_op jit(solution)/shard_map/ppermute | solution.py:282
  39.5 13.5 %collective-permute-start.2 = (bf16[4624,128]{1,0:T(8,128)(2,1)S(1)}, bf16[4624,128]{1,0:T(8,128)(2,1)S(1)}, u32[]{:S(2)}, u32[]{:S(2)}) collective-permute-start(bf16[4624,128]{1,0:T(8,128)(2,1)S(1)} %collective-permute-done.f), channel_id=1, source_target_pairs={{0,1},{1,0},{2,3},{3,2},{4,5},{5,4},{6,7},{7,6},{8,9},{9,8},{10,11... | collective-permute-start | bytes 3551240 | tf_op jit(solution)/shard_map/ppermute | solution.py:282
  49.2 9.9 %collective-permute-start.4 = (bf16[4624,128]{1,0:T(8,128)(2,1)S(1)}, bf16[4624,128]{1,0:T(8,128)(2,1)S(1)}, u32[]{:S(2)}, u32[]{:S(2)}) collective-permute-start(bf16[4624,128]{1,0:T(8,128)(2,1)S(1)} %collective-permute-done.3.g), channel_id=1, source_target_pairs={{0,1},{1,0},{2,3},{3,2},{4,5},{5,4},{6,7},{7,6},{8,9},{9,8},{10,11... | collective-permute-start | bytes 3551240 | tf_op jit(solution)/shard_map/ppermute | solution.py:282
  51.1 13.8 %collective-permute-start.5 = (bf16[2432,128]{1,0:T(8,128)(2,1)S(1)}, bf16[2432,128]{1,0:T(8,128)(2,1)S(1)}, u32[]{:S(2)}, u32[]{:S(2)}) collective-permute-start(bf16[2432,128]{1,0:T(8,128)(2,1)S(1)} %shard_map.31), channel_id=1, source_target_pairs={{0,511},{1,2},{2,1},{3,4},{4,3},{5,6},{6,5},{7,8},{8,7},{9,10},{10... | collective-permute-start | bytes 1867784 | tf_op jit(solution)/shard_map/ppermute | solution.py:282

commit v3 on v2

--- a/solution.py
+++ b/solution.py
@@ -17,6 +17,7 @@
 WIDE = SLOTS * TILE
 META = 16
 FULL = BODY + META
+LONG = FULL + META
 TALL = WIDE + TILE
 FAR = BAND + 1
 NEAR = BAND + 2
@@ -29,14 +30,17 @@
 FIND_AT = SLOT_AT + OWN
 STAGES = 3
 TILES_AT = FIND_AT + COLS * SPAN
-TABLE = TILES_AT + COLS * STAGES
+ODD_AT = TILES_AT + COLS * STAGES
+TABLE = ODD_AT + 1
 PAIR = 2 * TILE
 PAIRS = SLOTS // 2
 CHUNK = 256
+GROUP = 4
 BF16 = jnp.bfloat16
 F32 = jnp.float32
 ANY = pl.BlockSpec(memory_space=pl.ANY)
 VMEM = pl.BlockSpec(memory_space=pltpu.VMEM)
+HBM = pl.BlockSpec(memory_space=pltpu.HBM)
 SMEM = pl.BlockSpec(memory_space=pltpu.SMEM)
 
 
@@ -46,7 +50,7 @@
 
 def call(kernel, out_shape, in_specs, out_specs, scratch, aliases, micros, *args):
     args = [
-        pltpu.with_memory_space_constraint(arg, pltpu.VMEM) if spec is VMEM else arg
+        pltpu.with_memory_space_constraint(arg, spec.memory_space) if spec in (VMEM, HBM) else arg
         for arg, spec in zip(args, in_specs)
     ]
     return pl.pallas_call(
@@ -68,16 +72,28 @@
     return jnp.where(value < -(total // 2), value + total, value)
 
 
-def pack_kernel(total, device, rows, mine, packed, wide):
-    packed[pl.ds(0, BODY), :] = mine[...]
+def pack_kernel(total, device, rows, mine, packed, longer, near_rows, wide, sem):
+    copies = [
+        pltpu.make_async_copy(rows, near_rows, sem.at[0]),
+        pltpu.make_async_copy(mine, longer.at[pl.ds(0, BODY)], sem.at[1]),
+        pltpu.make_async_copy(mine, packed.at[pl.ds(0, BODY)], sem.at[2]),
+    ]
+    for copy in copies:
+        copy.start()
     column = device[0] * COLS + lax.broadcasted_iota(jnp.int32, (COLS, SLOTS), 0)
     wide[...] = jnp.zeros_like(wide)
-    wide[pl.ds(0, COLS), pl.ds(0, SLOTS)] = wrapped(rows[...] - column, total).astype(F32)
+    copies[0].wait()
+    wide[pl.ds(0, COLS), pl.ds(0, SLOTS)] = wrapped(near_rows[...] - column, total).astype(F32)
     packed[pl.ds(BODY, META), :] = wide[...].astype(BF16)
+    longer[pl.ds(BODY, META), :] = wide[...].astype(BF16)
+    longer[pl.ds(FULL, META), :] = jnp.zeros((META, TILE), BF16)
+    copies[1].wait()
+    copies[2].wait()
 
 
 def table_kernel(total, device, rows, table):
     odd = device[0] % 2
+    table[ODD_AT] = odd
     first = device[0] * COLS
     for c in range(COLS):
         for i in range(SPAN):
@@ -87,7 +103,8 @@
         for s in range(SLOTS):
             group = (places[s] + BAND + 1) // COLS
             group = jnp.where(odd == 1, 6 - group, group)
-            stage = jnp.where(group >= 3, jnp.maximum(group - 4, 0), 3 - group)
+            stage = jnp.where(group >= 3, jnp.maximum(group - 4, 0), group)
+            stage = jnp.where(group == 0, 3, stage)
             stages.append(stage)
             keys.append(stage * 16 + s)
         for s in range(SLOTS):
@@ -114,23 +131,21 @@
 
 
 def scatter(table, left, part, place, offset_at):
-    def one(i, carry):
-        j = i // COLS
-        c = i - j * COLS
-        here = FIND_AT + c * SPAN + SHIFT + place + j
-        k = table[here]
-
-        @pl.when(k < SLOTS)
-        def _():
-            for p in range(SLOTS):
-                s = table[here + offset_at(j, p)]
-                left[
-                    rows_at(c * TALL + s * TILE, TILE), rows_at(k * TILE, TILE)
-                ] = part[rows_at((j * SLOTS + p) * TILE, TILE), :]
-
-        return carry
-
-    lax.fori_loop(0, COLS * COLS, one, 0)
+    for j in range(part.shape[0] // WIDE):
+        for c in range(COLS):
+            here = FIND_AT + c * SPAN + SHIFT + place + j
+            k = table[here]
+
+            @pl.when(k < SLOTS)
+            def _():
+                for start in range(0, SLOTS, GROUP):
+                    taken = range(start, start + GROUP)
+                    to = [table[here + offset_at(j, p)] for p in taken]
+                    held = [part[rows_at((j * SLOTS + p) * TILE, TILE), :] for p in taken]
+                    for s, block in zip(to, held):
+                        left[
+                            rows_at(c * TALL + s * TILE, TILE), rows_at(k * TILE, TILE)
+                        ] = block
 
 
 def accumulate(left, right, total, c, low, high):
@@ -161,16 +176,14 @@
         refined = (3.0 * square[pl.ds(m, CHUNK), :].astype(F32) - 2.0 * cubed).astype(BF16)
         for i in range(CHUNK // TILE):
             slot = table[SLOT_AT + c * SLOTS + m // TILE + i]
-            result[rows_at(slot * TILE, TILE), :] = refined[i * TILE : (i + 1) * TILE]
-    copy = pltpu.make_async_copy(result, out.at[rows_at(c * WIDE, WIDE)], sem)
-    copy.start()
-    return copy
-
-
-def own_kernel(device, table, mine, x0, left, total, right, whole, offsets, sem):
-    side = 1 - 2 * (device[0] % 2)
-    copy = read_meta(x0, whole.at[0], offsets.at[0], sem.at[0])
-
+            here = rows_at(slot * TILE, TILE)
+            result[here, :] = refined[i * TILE : (i + 1) * TILE]
+            target = out.at[rows_at(c * WIDE + slot * TILE, TILE)]
+            pltpu.make_async_copy(result.at[here], target, sem).start()
+    return pltpu.make_async_copy(result, out.at[rows_at(c * WIDE, WIDE)], sem)
+
+
+def own_kernel(table, mine, left, total, right):
     def clear(i, carry):
         left[rows_at(i * TILE, TILE), :] = jnp.zeros((TILE, WIDE), BF16)
         return carry
@@ -187,35 +200,53 @@
 
     lax.fori_loop(0, OWN, order, 0)
     scatter(table, left, mine, 0, lambda j, p: table[PLACE_AT + j * SLOTS + p] - j)
-    copy.wait()
-    scatter(table, left, x0, 3 * side, lambda j, p: offsets[0, j, p])
-    for c in range(COLS):
-        accumulate(left, right, total, c, 0, tiles(table, c, 0))
-
-
-def outer_kernel(device, table, left_in, total_in, right, f, xf, left, total, whole, offsets, sem):
+
+
+def parts_kernel(places, low, high, table, left_in, total_in, right, *refs):
     del left_in, total_in
-    side = 1 - 2 * (device[0] % 2)
+    parts, (left, total, whole, offsets, sem) = refs[: len(places)], refs[len(places) :]
+    side = 1 - 2 * table[ODD_AT]
     copies = [
-        read_meta(part, whole.at[i], offsets.at[i], sem.at[i]) for i, part in enumerate((f, xf))
-    ]
-    for i, (part, place) in enumerate(((f, 6), (xf, -3))):
+        read_meta(part, whole.at[i], offsets.at[i], sem.at[i]) for i, part in enumerate(parts)
+    ]
+    for i, (part, place) in enumerate(zip(parts, places)):
         copies[i].wait()
         scatter(table, left, part, place * side, lambda j, p: offsets[i, j, p])
     for c in range(COLS):
-        accumulate(left, right, total, c, tiles(table, c, 0), tiles(table, c, 1))
+        accumulate(
+            left, right, total, c, 0 if low is None else tiles(table, c, low), tiles(table, c, high)
+        )
+
+
+def add_parts(table, left, total, right, parts, places, low, high, micros):
+    count = len(parts)
+    return call(
+        functools.partial(parts_kernel, places, low, high),
+        (pltpu.VMEM(left.shape, BF16), pltpu.VMEM(total.shape, F32)),
+        [SMEM] + [VMEM] * (3 + count),
+        (VMEM, VMEM),
+        [*meta_scratch(count), pltpu.SemaphoreType.DMA((count,))],
+        {1: 0, 2: 1},
+        micros,
+        table,
+        left,
+        total,
+        right,
+        *parts,
+    )
 
 
 def early_kernel(
-    device, table, left_in, total_in, right, g, xg, left, total, out, whole, offsets, square, result, sem
+    table, left_in, total_in, right, x, left, total, out, whole, offsets, square, result, sem
 ):
     del left_in, total_in
-    odd = device[0] % 2
+    odd = table[ODD_AT]
     side = 1 - 2 * odd
+    parts = [x.at[pl.ds(i * LONG, LONG)] for i in range(2)]
     copies = [
-        read_meta(part, whole.at[i], offsets.at[i], sem.at[i]) for i, part in enumerate((g, xg))
-    ]
-    for i, (part, place) in enumerate(((g, -6), (xg, 9))):
+        read_meta(part, whole.at[i], offsets.at[i], sem.at[i]) for i, part in enumerate(parts)
+    ]
+    for i, (part, place) in enumerate(zip(parts, (-3, 9))):
         copies[i].wait()
         scatter(table, left, part, place * side, lambda j, p: offsets[i, j, p])
     first = 2 - 2 * odd
@@ -227,10 +258,10 @@
 
 
 def last_kernel(
-    device, table, left_in, total_in, right, relay, out_in, left, total, out, square, result, sem
+    table, left_in, total_in, right, relay, out_in, left, total, out, square, result, sem
 ):
     del left_in, total_in, out_in
-    odd = device[0] % 2
+    odd = table[ODD_AT]
     copies = []
     for i, c in enumerate((1, 2 * odd)):
         for start, size, place, low in (
@@ -254,9 +285,15 @@
         copy.wait()
 
 
-def relay_kernel(device, f, relay, whole, offsets, sem):
-    odd = device[0] % 2
-    copy = read_meta(f, whole, offsets, sem)
+def relay_kernel(table, f, g, relay, joined, whole, offsets, sem):
+    odd = table[ODD_AT]
+    copy = read_meta(f, whole, offsets, sem.at[0])
+    joins = [
+        pltpu.make_async_copy(part, joined.at[pl.ds(i * LONG, LONG)], sem.at[1 + i])
+        for i, part in enumerate((f, g))
+    ]
+    for join in joins:
+        join.start()
     relay[...] = jnp.zeros_like(relay)
     copy.wait()
     for column, start, size, shift in (
@@ -276,6 +313,8 @@
             return carry
 
         lax.fori_loop(0, SLOTS, one, 0)
+    for join in joins:
+        join.wait()
 
 
 def send(value, pairs):
@@ -305,23 +344,25 @@
 
     mine = blocks.reshape(BODY, TILE)
     device = device.astype(jnp.int32).reshape(1)
-    packed = call(
+    packed, longer = call(
         functools.partial(pack_kernel, columns),
-        pltpu.VMEM((FULL, TILE), BF16),
-        [SMEM, VMEM, VMEM],
-        VMEM,
-        [pltpu.VMEM((META, TILE), F32)],
+        (pltpu.VMEM((FULL, TILE), BF16), pltpu.VMEM((LONG, TILE), BF16)),
+        [SMEM, HBM, HBM],
+        (VMEM, VMEM),
+        [
+            pltpu.VMEM((COLS, SLOTS), jnp.int32),
+            pltpu.VMEM((META, TILE), F32),
+            pltpu.SemaphoreType.DMA((3,)),
+        ],
         {},
         1,
         device,
         block_rows,
         mine,
     )
-    f = send(packed, outward)
     x0 = send(packed, across)
-    packed, x0 = after(packed, x0)
-    g = send(packed, inward)
-
+    f = send(longer, outward)
+    g = send(longer, inward)
     table = call(
         functools.partial(table_kernel, columns),
         jax.ShapeDtypeStruct((TABLE,), jnp.int32),
@@ -339,58 +380,40 @@
     left, total, right = call(
         own_kernel,
         (left_shape, total_shape, pltpu.VMEM((BODY, TILE), BF16)),
-        [SMEM, SMEM, VMEM, VMEM],
+        [SMEM, VMEM],
         (VMEM, VMEM, VMEM),
-        [*meta_scratch(1), pltpu.SemaphoreType.DMA((1,))],
+        [],
         {},
-        6,
-        device,
+        8,
         table,
-        mine,
-        x0,
-    )
-
+        packed,
+    )
+    left, total = add_parts(table, left, total, right, (x0,), (3,), None, 0, 4)
     f, left = after(f, left)
-    relay = call(
+    relay, joined = call(
         relay_kernel,
-        pltpu.VMEM((RELAY * TILE, TILE), BF16),
-        [SMEM, VMEM],
-        VMEM,
+        (pltpu.VMEM((RELAY * TILE, TILE), BF16), pltpu.VMEM((2 * LONG, TILE), BF16)),
+        [SMEM, VMEM, VMEM],
+        (VMEM, VMEM),
         [
             pltpu.VMEM((META, TILE), jnp.int32),
             pltpu.SMEM((META, TILE), jnp.int32),
-            pltpu.SemaphoreType.DMA,
+            pltpu.SemaphoreType.DMA((3,)),
         ],
         {},
         1,
-        device,
+        table,
         f,
-    )
-    f, relay = after(f, relay)
+        g,
+    )
     relay = send(relay, onward)
-    xf = send(f, across)
-    xg = send(g, across)
-    xf, g = after(xf, g)
-    left, total = call(
-        outer_kernel,
-        (left_shape, total_shape),
-        [SMEM, SMEM] + [VMEM] * 5,
-        (VMEM, VMEM),
-        [*meta_scratch(2), pltpu.SemaphoreType.DMA((2,))],
-        {2: 0, 3: 1},
-        4,
-        device,
-        table,
-        left,
-        total,
-        right,
-        f,
-        xf,
-    )
+    x = send(joined, across)
+    left, total = add_parts(table, left, total, right, (f, g), (6, -6), 0, 1, 4)
+    x, left = after(x, left)
     left, total, out = call(
         early_kernel,
         (left_shape, total_shape, out_shape),
-        [SMEM, SMEM] + [VMEM] * 5,
+        [SMEM] + [VMEM] * 4,
         (VMEM, VMEM, ANY),
         [
             *meta_scratch(2),
@@ -398,29 +421,26 @@
             pltpu.VMEM((WIDE, TILE), BF16),
             pltpu.SemaphoreType.DMA((3,)),
         ],
-        {2: 0, 3: 1},
+        {1: 0, 2: 1},
         4,
-        device,
         table,
         left,
         total,
         right,
-        g,
-        xg,
+        x,
     )
     out = call(
         last_kernel,
         (left_shape, total_shape, out_shape),
-        [SMEM, SMEM] + [VMEM] * 4 + [ANY],
+        [SMEM] + [VMEM] * 4 + [ANY],
         (VMEM, VMEM, ANY),
         [
             pltpu.VMEM((WIDE, TILE), BF16),
             pltpu.VMEM((2, WIDE, TILE), BF16),
             pltpu.SemaphoreType.DMA((2,)),
         ],
-        {2: 0, 3: 1, 6: 2},
+        {1: 0, 2: 1, 5: 2},
         4,
-        device,
         table,
         left,
         total,

time: 70.2 us -> 67.6 us (0.963); the launches traced: 69.9 us -> 66.5 us
  starting transfers between devices: 34.7 us -> 25.2 us
  waiting for transfers between devices: 6.69 us -> 12.8 us
  local copies, waits for them, and re-layouts: 1.95 us -> 0.68 us
  Pallas kernels: 26.5 us -> 27.5 us
    ppermute x6 -> x5, starting transfers between devices: 34.7 us -> 25.2 us  [send(): return lax.ppermute(value, AXES, pairs)]
    ppermute x6 -> x5, waiting for transfers between devices: 6.69 us -> 12.8 us  [send(): return lax.ppermute(value, AXES, pairs)]
    unnamed x6 -> x2, local copies, waits for them, and re-layouts: 1.95 us -> 0.68 us
    pallas_call x7 -> x8, Pallas kernels: 26.5 us -> 27.5 us  [call(): pl.pallas_call(kernel, out_shape=out_shape, in_specs=in_specs, out_specs=...]
  transfers between devices with their start and end apart: 6 -> 5, of which waited for: 2 -> 2; matrix products, arithmetic and copies ran while one was open for 0% -> 0% of each run, Pallas kernels for 31% -> 28%
where the time goes in v3:
time: 67.6 us; the launch traced here: 66.5 us
  Pallas kernels  27.5 us (41%)
  starting transfers between devices  25.2 us (37%)
  waiting for transfers between devices  12.8 us (19%)
  local copies, waits for them, and re-layouts  0.68 us (1%)
    pallas_call x8, Pallas kernels, call(): pl.pallas_call(kernel, out_shape=out_shape, in_specs=in_specs, out_specs=...  27.5 us
    ppermute x5, starting transfers between devices, send(): return lax.ppermute(value, AXES, pairs)  25.2 us
    ppermute x5, waiting for transfers between devices, send(): return lax.ppermute(value, AXES, pairs)  12.8 us
  transfers between devices with their start and end apart: 5, of which 2 were waited for; matrix products, arithmetic and copies ran while one was open for 0% of the time, Pallas kernels for 28%

profile of v3, /device:TPU:1, one launch (start us, length us, event | category | flops | bytes accessed | tf_op | source)
XLA Modules:
  0.0 66.5 jit_solution(4801800667623254893)
XLA Ops:
  0.0 1.7 %shard_map.29 = (bf16[4624,128]{1,0:T(8,128)(2,1)S(1)}, bf16[4640,128]{1,0:T(8,128)(2,1)S(1)}) custom-call(s32[1]{0:T(128)} %bitcast.device, s32[3,12]{1,0:T(4,128)} %rows.3, bf16[4608,128]{1,0:T(8,128)(2,1)} %bitcast.3), custom_call_target="tpu_custom_call" | custom-call | bytes 3000000 | tf_op jit(solution)/shard_map/pallas_call | solution.py:56
  1.7 4.0 %collective-permute-start = (bf16[4640,128]{1,0:T(8,128)(2,1)S(1)}, bf16[4640,128]{1,0:T(8,128)(2,1)S(1)}, u32[]{:S(2)}, u32[]{:S(2)}) collective-permute-start(bf16[4640,128]{1,0:T(8,128)(2,1)S(1)} %get-tuple-element.24), channel_id=1, source_target_pairs={{0,510},{1,3},{2,0},{3,5},{4,2},{5,7},{6,4},{7,9},{8,6},{9,11},{10... | collective-permute-start | bytes 3563528 | tf_op jit(solution)/shard_map/ppermute | solution.py:321
  5.8 14.5 %collective-permute-start.2 = (bf16[4640,128]{1,0:T(8,128)(2,1)S(1)}, bf16[4640,128]{1,0:T(8,128)(2,1)S(1)}, u32[]{:S(2)}, u32[]{:S(2)}) collective-permute-start(bf16[4640,128]{1,0:T(8,128)(2,1)S(1)} %get-tuple-element.24), channel_id=1, source_target_pairs={{0,2},{1,511},{2,4},{3,1},{4,6},{5,3},{6,8},{7,5},{8,10},{9,7},{10... | collective-permute-start | bytes 3563528 | tf_op jit(solution)/shard_map/ppermute | solution.py:321
  20.3 2.9 %collective-permute-start.1 = (bf16[4624,128]{1,0:T(8,128)(2,1)S(1)}, bf16[4624,128]{1,0:T(8,128)(2,1)S(1)}, u32[]{:S(2)}, u32[]{:S(2)}) collective-permute-start(bf16[4624,128]{1,0:T(8,128)(2,1)S(1)} %get-tuple-element.25.mine), channel_id=1, source_target_pairs={{0,1},{1,0},{2,3},{3,2},{4,5},{5,4},{6,7},{7,6},{8,9},{9,8},{10,11... | collective-permute-start | bytes 3551240 | tf_op jit(solution)/shard_map/ppermute | solution.py:321
  23.1 0.0 copy-start
  23.2 0.7 %copy-done = s32[3,12]{1,0:T(4,128)S(1)} copy-done((s32[3,12]{1,0:T(4,128)S(1)}, s32[3,12]{1,0:T(4,128)}, u32[]{:S(2)}) %copy-start) | copy-done | bytes 168
  23.8 2.2 %shard_map.28.table = s32[238]{0:T(256)S(1)} custom-call(s32[1]{0:T(128)} %bitcast.device, s32[3,12]{1,0:T(4,128)S(1)} %copy-done), custom_call_target="tpu_custom_call" | custom-call | bytes 6000000 | tf_op jit(solution)/shard_map/pallas_call | solution.py:56
  26.1 3.0 %shard_map.30 = (bf16[4992,1536]{1,0:T(8,128)(2,1)S(1)}, f32[4608,128]{1,0:T(8,128)S(1)}, bf16[4608,128]{1,0:T(8,128)(2,1)S(1)}) custom-call(s32[238]{0:T(256)S(1)} %shard_map.28.table, bf16[4624,128]{1,0:T(8,128)(2,1)S(1)} %get-tuple-element.25.mine), custom_call_target="tpu_custom_call" | custom-call | bytes 24000000 | tf_op jit(solution)/shard_map/pallas_call | solution.py:56
  29.1 0.0 collective-permute-done.1.refs_0_
  29.1 3.5 %shard_map.31 = (bf16[4992,1536]{1,0:T(8,128)(2,1)S(1)}, f32[4608,128]{1,0:T(8,128)S(1)}) custom-call(s32[238]{0:T(256)S(1)} %shard_map.28.table, bf16[4992,1536]{1,0:T(8,128)(2,1)S(1)} %get-tuple-element.26.left_in, f32[4608,128]{1,0:T(8,128)S(1)} %get-tuple-element.27.total_in, ...), custom_call_target="tpu_custom_call", output_to_operand_aliasing={{0}: (1, {}), {1}: (2, {})} | custom-call | bytes 12000000 | tf_op jit(solution)/shard_map/pallas_call | solution.py:56
  32.6 2.1 %collective-permute-done.f.refs_0_ = bf16[4640,128]{1,0:T(8,128)(2,1)S(1)} collective-permute-done((bf16[4640,128]{1,0:T(8,128)(2,1)S(1)}, bf16[4640,128]{1,0:T(8,128)(2,1)S(1)}, u32[]{:S(2)}, u32[]{:S(2)}) %collective-permute-start) | collective-permute-done | bytes 1187872 | tf_op jit(solution)/shard_map/ppermute | solution.py:321
  34.7 10.7 %collective-permute-done.2.g.refs_1_ = bf16[4640,128]{1,0:T(8,128)(2,1)S(1)} collective-permute-done((bf16[4640,128]{1,0:T(8,128)(2,1)S(1)}, bf16[4640,128]{1,0:T(8,128)(2,1)S(1)}, u32[]{:S(2)}, u32[]{:S(2)}) %collective-permute-start.2) | collective-permute-done | bytes 1187872 | tf_op jit(solution)/shard_map/ppermute | solution.py:321
  45.4 1.7 %shard_map.32 = (bf16[2432,128]{1,0:T(8,128)(2,1)S(1)}, bf16[9280,128]{1,0:T(8,128)(2,1)S(1)}) custom-call(s32[238]{0:T(256)S(1)} %shard_map.28.table, bf16[4640,128]{1,0:T(8,128)(2,1)S(1)} %collective-permute-done.f.refs_0_, bf16[4640,128]{1,0:T(8,128)(2,1)S(1)} %collective-permute-done.2.g.refs_1_), custom_call_target="tpu_custom_call" | custom-call | bytes 3000000 | tf_op jit(solution)/shard_map/pallas_call | solution.py:56
  47.1 1.9 %collective-permute-start.3 = (bf16[9280,128]{1,0:T(8,128)(2,1)S(1)}, bf16[9280,128]{1,0:T(8,128)(2,1)S(1)}, u32[]{:S(2)}, u32[]{:S(2)}) collective-permute-start(bf16[9280,128]{1,0:T(8,128)(2,1)S(1)} %get-tuple-element.31), channel_id=1, source_target_pairs={{0,1},{1,0},{2,3},{3,2},{4,5},{5,4},{6,7},{7,6},{8,9},{9,8},{10,11... | collective-permute-start | bytes 7127048 | tf_op jit(solution)/shard_map/ppermute | solution.py:321
  49.0 1.9 %collective-permute-start.4 = (bf16[2432,128]{1,0:T(8,128)(2,1)S(1)}, bf16[2432,128]{1,0:T(8,128)(2,1)S(1)}, u32[]{:S(2)}, u32[]{:S(2)}) collective-permute-start(bf16[2432,128]{1,0:T(8,128)(2,1)S(1)} %get-tuple-element.40), channel_id=1, source_target_pairs={{0,511},{1,2},{2,1},{3,4},{4,3},{5,6},{6,5},{7,8},{8,7},{9,10},{10... | collective-permute-start | bytes 1867784 | tf_op jit(solution)/shard_map/ppermute | solution.py:321
  51.0 5.0 %shard_map.33 = (bf16[4992,1536]{1,0:T(8,128)(2,1)S(1)}, f32[4608,128]{1,0:T(8,128)S(1)}) custom-call(s32[238]{0:T(256)S(1)} %shard_map.28.table, bf16[4992,1536]{1,0:T(8,128)(2,1)S(1)} %get-tuple-element.32.left_in, f32[4608,128]{1,0:T(8,128)S(1)} %get-tuple-element.33.total_in, ...), custom_call_target="tpu_custom_call", output_to_operand_aliasing={{0}: (1, {}), {1}: (2, {})} | custom-call | bytes 12000000 | tf_op jit(solution)/shard_map/pallas_call | solution.py:56
  56.0 0.0 collective-permute-done.3.x
  56.0 5.0 %shard_map.34 = (bf16[4992,1536]{1,0:T(8,128)(2,1)S(1)}, f32[4608,128]{1,0:T(8,128)S(1)}, bf16[4608,128]{1,0:T(8,128)(2,1)}) custom-call(s32[238]{0:T(256)S(1)} %shard_map.28.table, bf16[4992,1536]{1,0:T(8,128)(2,1)S(1)} %get-tuple-element.35.left_in, f32[4608,128]{1,0:T(8,128)S(1)} %get-tuple-element.36.total_in, ...), custom_call_target="tpu_custom_call", output_to_operand_aliasing={{0}: (1, {}), {1}: (2, {})} | custom-call | bytes 12000000 | tf_op jit(solution)/shard_map/pallas_call | solution.py:56
  61.0 0.0 collective-permute-done.4.relay
  61.1 5.3 %shard_map.35 = (bf16[4992,1536]{1,0:T(8,128)(2,1)S(1)}, f32[4608,128]{1,0:T(8,128)S(1)}, bf16[4608,128]{1,0:T(8,128)(2,1)}) custom-call(s32[238]{0:T(256)S(1)} %shard_map.28.table, bf16[4992,1536]{1,0:T(8,128)(2,1)S(1)} %get-tuple-element.38.left_in, ...), custom_call_target="tpu_custom_call", output_to_operand_aliasing={{0}: (1, {}), {1}: (2, {}), {2}: (5, {})} | custom-call | bytes 12000000 | tf_op jit(solution)/shard_map/pallas_call | solution.py:56
Async XLA Ops:
  1.7 33.0 %collective-permute-start = (bf16[4640,128]{1,0:T(8,128)(2,1)S(1)}, bf16[4640,128]{1,0:T(8,128)(2,1)S(1)}, u32[]{:S(2)}, u32[]{:S(2)}) collective-permute-start(bf16[4640,128]{1,0:T(8,128)(2,1)S(1)} %get-tuple-element.24), channel_id=1, source_target_pairs={{0,510},{1,3},{2,0},{3,5},{4,2},{5,7},{6,4},{7,9},{8,6},{9,11},{10... | collective-permute-start | bytes 3563528 | tf_op jit(solution)/shard_map/ppermute | solution.py:321
  5.8 39.6 %collective-permute-start.2 = (bf16[4640,128]{1,0:T(8,128)(2,1)S(1)}, bf16[4640,128]{1,0:T(8,128)(2,1)S(1)}, u32[]{:S(2)}, u32[]{:S(2)}) collective-permute-start(bf16[4640,128]{1,0:T(8,128)(2,1)S(1)} %get-tuple-element.24), channel_id=1, source_target_pairs={{0,2},{1,511},{2,4},{3,1},{4,6},{5,3},{6,8},{7,5},{8,10},{9,7},{10... | collective-permute-start | bytes 3563528 | tf_op jit(solution)/shard_map/ppermute | solution.py:321
  20.3 8.8 %collective-permute-start.1 = (bf16[4624,128]{1,0:T(8,128)(2,1)S(1)}, bf16[4624,128]{1,0:T(8,128)(2,1)S(1)}, u32[]{:S(2)}, u32[]{:S(2)}) collective-permute-start(bf16[4624,128]{1,0:T(8,128)(2,1)S(1)} %get-tuple-element.25.mine), channel_id=1, source_target_pairs={{0,1},{1,0},{2,3},{3,2},{4,5},{5,4},{6,7},{7,6},{8,9},{9,8},{10,11... | collective-permute-start | bytes 3551240 | tf_op jit(solution)/shard_map/ppermute | solution.py:321
  23.1 0.7 %copy-start = (s32[3,12]{1,0:T(4,128)S(1)}, s32[3,12]{1,0:T(4,128)}, u32[]{:S(2)}) copy-start(s32[3,12]{1,0:T(4,128)} %rows.3) | copy-start | bytes 436
  47.1 8.9 %collective-permute-start.3 = (bf16[9280,128]{1,0:T(8,128)(2,1)S(1)}, bf16[9280,128]{1,0:T(8,128)(2,1)S(1)}, u32[]{:S(2)}, u32[]{:S(2)}) collective-permute-start(bf16[9280,128]{1,0:T(8,128)(2,1)S(1)} %get-tuple-element.31), channel_id=1, source_target_pairs={{0,1},{1,0},{2,3},{3,2},{4,5},{5,4},{6,7},{7,6},{8,9},{9,8},{10,11... | collective-permute-start | bytes 7127048 | tf_op jit(solution)/shard_map/ppermute | solution.py:321
  49.0 12.0 %collective-permute-start.4 = (bf16[2432,128]{1,0:T(8,128)(2,1)S(1)}, bf16[2432,128]{1,0:T(8,128)(2,1)S(1)}, u32[]{:S(2)}, u32[]{:S(2)}) collective-permute-start(bf16[2432,128]{1,0:T(8,128)(2,1)S(1)} %get-tuple-element.40), channel_id=1, source_target_pairs={{0,511},{1,2},{2,1},{3,4},{4,3},{5,6},{6,5},{7,8},{8,7},{9,10},{10... | collective-permute-start | bytes 1867784 | tf_op jit(solution)/shard_map/ppermute | solution.py:321

commit v4 on v3

--- a/solution.py
+++ b/solution.py
@@ -72,23 +72,24 @@
     return jnp.where(value < -(total // 2), value + total, value)
 
 
-def pack_kernel(total, device, rows, mine, packed, longer, near_rows, wide, sem):
-    copies = [
-        pltpu.make_async_copy(rows, near_rows, sem.at[0]),
-        pltpu.make_async_copy(mine, longer.at[pl.ds(0, BODY)], sem.at[1]),
-        pltpu.make_async_copy(mine, packed.at[pl.ds(0, BODY)], sem.at[2]),
-    ]
-    for copy in copies:
-        copy.start()
+def pack_kernel(total, device, rows, mine, longer, near_rows, wide, sem):
+    body = pltpu.make_async_copy(mine, longer.at[pl.ds(0, BODY)], sem.at[0])
+    lists = pltpu.make_async_copy(rows, near_rows, sem.at[1])
+    body.start()
+    lists.start()
     column = device[0] * COLS + lax.broadcasted_iota(jnp.int32, (COLS, SLOTS), 0)
     wide[...] = jnp.zeros_like(wide)
-    copies[0].wait()
+    longer[pl.ds(FULL, META), :] = jnp.zeros((META, TILE), BF16)
+    lists.wait()
     wide[pl.ds(0, COLS), pl.ds(0, SLOTS)] = wrapped(near_rows[...] - column, total).astype(F32)
-    packed[pl.ds(BODY, META), :] = wide[...].astype(BF16)
     longer[pl.ds(BODY, META), :] = wide[...].astype(BF16)
-    longer[pl.ds(FULL, META), :] = jnp.zeros((META, TILE), BF16)
-    copies[1].wait()
-    copies[2].wait()
+    body.wait()
+
+
+def shorten_kernel(longer, packed, sem):
+    copy = pltpu.make_async_copy(longer.at[pl.ds(0, FULL)], packed, sem)
+    copy.start()
+    copy.wait()
 
 
 def table_kernel(total, device, rows, table):
@@ -246,6 +247,8 @@
     copies = [
         read_meta(part, whole.at[i], offsets.at[i], sem.at[i]) for i, part in enumerate(parts)
     ]
+    for c in range(COLS):
+        accumulate(left, right, total, c, tiles(table, c, 0), tiles(table, c, 1))
     for i, (part, place) in enumerate(zip(parts, (-3, 9))):
         copies[i].wait()
         scatter(table, left, part, place * side, lambda j, p: offsets[i, j, p])
@@ -285,20 +288,11 @@
         copy.wait()
 
 
-def relay_kernel(table, f, g, relay, joined, whole, offsets, sem):
-    odd = table[ODD_AT]
-    copy = read_meta(f, whole, offsets, sem.at[0])
-    joins = [
-        pltpu.make_async_copy(part, joined.at[pl.ds(i * LONG, LONG)], sem.at[1 + i])
-        for i, part in enumerate((f, g))
-    ]
-    for join in joins:
-        join.start()
+def fill_relay(odd, f, relay, offsets):
     relay[...] = jnp.zeros_like(relay)
-    copy.wait()
     for column, start, size, shift in (
-        (1, 0, FAR, jnp.where(odd == 1, 0, BAND)),
-        (2 * odd, FAR, NEAR, jnp.where(odd == 1, 1, BAND)),
+        (1, 0, FAR, 0 if odd else BAND),
+        (2 * odd, FAR, NEAR, 1 if odd else BAND),
     ):
 
         def one(p, carry):
@@ -313,8 +307,51 @@
             return carry
 
         lax.fori_loop(0, SLOTS, one, 0)
+
+
+def odd_kernel(table, f, left_in, relay, left, whole, offsets, sem):
+    del left_in
+
+    @pl.when(table[ODD_AT] == 1)
+    def _():
+        read_meta(f, whole, offsets, sem).wait()
+        fill_relay(1, f, relay, offsets)
+        scatter(table, left, f, -6, lambda j, p: offsets[j, p])
+
+
+def even_kernel(device, f, relay_in, relay, whole, offsets, sem):
+    del relay_in
+
+    @pl.when(device[0] % 2 == 0)
+    def _():
+        read_meta(f, whole, offsets, sem).wait()
+        fill_relay(0, f, relay, offsets)
+
+
+def join_kernel(f, g, joined, sem):
+    joins = [
+        pltpu.make_async_copy(part, joined.at[pl.ds(i * LONG, LONG)], sem.at[i])
+        for i, part in enumerate((f, g))
+    ]
+    for join in joins:
+        join.start()
     for join in joins:
         join.wait()
+
+
+def near_kernel(table, left_in, f, g, left, whole, offsets, sem):
+    del left_in
+    odd = table[ODD_AT]
+    copies = [
+        read_meta(part, whole.at[i], offsets.at[i], sem.at[i]) for i, part in enumerate((g, f))
+    ]
+    for copy in copies:
+        copy.wait()
+    scatter(table, left, g, 12 * odd - 6, lambda j, p: offsets[0, j, p])
+
+    @pl.when(odd == 0)
+    def _():
+        scatter(table, left, f, 6, lambda j, p: offsets[1, j, p])
 
 
 def send(value, pairs):
@@ -344,21 +381,31 @@
 
     mine = blocks.reshape(BODY, TILE)
     device = device.astype(jnp.int32).reshape(1)
-    packed, longer = call(
+    longer = call(
         functools.partial(pack_kernel, columns),
-        (pltpu.VMEM((FULL, TILE), BF16), pltpu.VMEM((LONG, TILE), BF16)),
+        pltpu.VMEM((LONG, TILE), BF16),
         [SMEM, HBM, HBM],
-        (VMEM, VMEM),
+        VMEM,
         [
             pltpu.VMEM((COLS, SLOTS), jnp.int32),
             pltpu.VMEM((META, TILE), F32),
-            pltpu.SemaphoreType.DMA((3,)),
+            pltpu.SemaphoreType.DMA((2,)),
         ],
         {},
         1,
         device,
         block_rows,
         mine,
+    )
+    packed = call(
+        shorten_kernel,
+        pltpu.VMEM((FULL, TILE), BF16),
+        [VMEM],
+        VMEM,
+        [pltpu.SemaphoreType.DMA],
+        {},
+        1,
+        longer,
     )
     x0 = send(packed, across)
     f = send(longer, outward)
@@ -390,25 +437,67 @@
     )
     left, total = add_parts(table, left, total, right, (x0,), (3,), None, 0, 4)
     f, left = after(f, left)
-    relay, joined = call(
-        relay_kernel,
-        (pltpu.VMEM((RELAY * TILE, TILE), BF16), pltpu.VMEM((2 * LONG, TILE), BF16)),
+    relay_shape = pltpu.VMEM((RELAY * TILE, TILE), BF16)
+    relay, left = call(
+        odd_kernel,
+        (relay_shape, left_shape),
         [SMEM, VMEM, VMEM],
         (VMEM, VMEM),
         [
             pltpu.VMEM((META, TILE), jnp.int32),
             pltpu.SMEM((META, TILE), jnp.int32),
-            pltpu.SemaphoreType.DMA((3,)),
+            pltpu.SemaphoreType.DMA,
         ],
-        {},
+        {2: 1},
         1,
         table,
         f,
+        left,
+    )
+    g, left = after(g, left)
+    joined = call(
+        join_kernel,
+        pltpu.VMEM((2 * LONG, TILE), BF16),
+        [VMEM, VMEM],
+        VMEM,
+        [pltpu.SemaphoreType.DMA((2,))],
+        {},
+        1,
+        f,
         g,
     )
+    x = send(joined, across)
+    relay, joined = after(relay, joined)
+    relay = call(
+        even_kernel,
+        relay_shape,
+        [SMEM, VMEM, VMEM],
+        VMEM,
+        [
+            pltpu.VMEM((META, TILE), jnp.int32),
+            pltpu.SMEM((META, TILE), jnp.int32),
+            pltpu.SemaphoreType.DMA,
+        ],
+        {2: 0},
+        1,
+        device,
+        f,
+        relay,
+    )
     relay = send(relay, onward)
-    x = send(joined, across)
-    left, total = add_parts(table, left, total, right, (f, g), (6, -6), 0, 1, 4)
+    left = call(
+        near_kernel,
+        left_shape,
+        [SMEM] + [VMEM] * 3,
+        VMEM,
+        [*meta_scratch(2), pltpu.SemaphoreType.DMA((2,))],
+        {1: 0},
+        4,
+        table,
+        left,
+        f,
+        g,
+    )
     x, left = after(x, left)
     left, total, out = call(
         early_kernel,

time: 67.6 us -> 65.6 us (0.970)
  waiting for transfers between devices: 12.8 us -> 11.7 us
    ppermute x5, waiting for transfers between devices: 12.8 us -> 11.7 us  [send(): return lax.ppermute(value, AXES, pairs)]
    pallas_call x8 -> x11, Pallas kernels: 27.5 us -> 27.3 us  [call(): pl.pallas_call(kernel, out_shape=out_shape, in_specs=in_specs, out_specs=...]
  transfers between devices with their start and end apart: 5 -> 5, of which waited for: 2 -> 4; matrix products, arithmetic and copies ran while one was open for 0% -> 0% of each run, Pallas kernels for 28% -> 32%
where the time goes in v4:
time: 65.6 us; the launch traced here: 64.7 us
  Pallas kernels  27.3 us (42%)
  starting transfers between devices  25.4 us (39%)
  waiting for transfers between devices  11.7 us (18%)
    pallas_call x11, Pallas kernels, call(): pl.pallas_call(kernel, out_shape=out_shape, in_specs=in_specs, out_specs=...  27.3 us
    ppermute x5, starting transfers between devices, send(): return lax.ppermute(value, AXES, pairs)  25.4 us
    ppermute x5, waiting for transfers between devices, send(): return lax.ppermute(value, AXES, pairs)  11.7 us
  transfers between devices with their start and end apart: 5, of which 4 were waited for; matrix products, arithmetic and copies ran while one was open for 0% of the time, Pallas kernels for 32%

profile of v4, /device:TPU:1, one launch (start us, length us, event | category | flops | bytes accessed | tf_op | source)
XLA Modules:
  0.0 64.7 jit_solution(18356484725688489547)
XLA Ops:
  0.0 0.0 copy-start
  0.0 1.3 %shard_map.29.longer = bf16[4640,128]{1,0:T(8,128)(2,1)S(1)} custom-call(s32[1]{0:T(128)} %bitcast.device, s32[3,12]{1,0:T(4,128)} %rows.3, bf16[4608,128]{1,0:T(8,128)(2,1)} %bitcast.3), custom_call_target="tpu_custom_call" | custom-call | bytes 3000000 | tf_op jit(solution)/shard_map/pallas_call | solution.py:56
  1.3 4.0 %collective-permute-start = (bf16[4640,128]{1,0:T(8,128)(2,1)S(1)}, bf16[4640,128]{1,0:T(8,128)(2,1)S(1)}, u32[]{:S(2)}, u32[]{:S(2)}) collective-permute-start(bf16[4640,128]{1,0:T(8,128)(2,1)S(1)} %shard_map.29.longer), channel_id=1, source_target_pairs={{0,510},{1,3},{2,0},{3,5},{4,2},{5,7},{6,4},{7,9},{8,6},{9,11},{10... | collective-permute-start | bytes 3563528 | tf_op jit(solution)/shard_map/ppermute | solution.py:358
  5.4 14.5 %collective-permute-start.2 = (bf16[4640,128]{1,0:T(8,128)(2,1)S(1)}, bf16[4640,128]{1,0:T(8,128)(2,1)S(1)}, u32[]{:S(2)}, u32[]{:S(2)}) collective-permute-start(bf16[4640,128]{1,0:T(8,128)(2,1)S(1)} %shard_map.29.longer), channel_id=1, source_target_pairs={{0,2},{1,511},{2,4},{3,1},{4,6},{5,3},{6,8},{7,5},{8,10},{9,7},{10... | collective-permute-start | bytes 3563528 | tf_op jit(solution)/shard_map/ppermute | solution.py:358
  19.8 0.3 shard_map.30.mine
  20.1 2.9 %collective-permute-start.1 = (bf16[4624,128]{1,0:T(8,128)(2,1)S(1)}, bf16[4624,128]{1,0:T(8,128)(2,1)S(1)}, u32[]{:S(2)}, u32[]{:S(2)}) collective-permute-start(bf16[4624,128]{1,0:T(8,128)(2,1)S(1)} %shard_map.30.mine), channel_id=1, source_target_pairs={{0,1},{1,0},{2,3},{3,2},{4,5},{5,4},{6,7},{7,6},{8,9},{9,8},{10,11... | collective-permute-start | bytes 3551240 | tf_op jit(solution)/shard_map/ppermute | solution.py:358
  23.0 0.0 copy-done
  23.0 2.2 %shard_map.28.table = s32[238]{0:T(256)S(1)} custom-call(s32[1]{0:T(128)} %bitcast.device, s32[3,12]{1,0:T(4,128)S(1)} %copy-done), custom_call_target="tpu_custom_call" | custom-call | bytes 6000000 | tf_op jit(solution)/shard_map/pallas_call | solution.py:56
  25.2 3.0 %shard_map.31 = (bf16[4992,1536]{1,0:T(8,128)(2,1)S(1)}, f32[4608,128]{1,0:T(8,128)S(1)}, bf16[4608,128]{1,0:T(8,128)(2,1)S(1)}) custom-call(s32[238]{0:T(256)S(1)} %shard_map.28.table, bf16[4624,128]{1,0:T(8,128)(2,1)S(1)} %shard_map.30.mine), custom_call_target="tpu_custom_call" | custom-call | bytes 24000000 | tf_op jit(solution)/shard_map/pallas_call | solution.py:56
  28.2 0.0 collective-permute-done.1.refs_0_
  28.2 3.1 %shard_map.32 = (bf16[4992,1536]{1,0:T(8,128)(2,1)S(1)}, f32[4608,128]{1,0:T(8,128)S(1)}) custom-call(s32[238]{0:T(256)S(1)} %shard_map.28.table, bf16[4992,1536]{1,0:T(8,128)(2,1)S(1)} %get-tuple-element.23.left_in, f32[4608,128]{1,0:T(8,128)S(1)} %get-tuple-element.24.total_in, ...), custom_call_target="tpu_custom_call", output_to_operand_aliasing={{0}: (1, {}), {1}: (2, {})} | custom-call | bytes 12000000 | tf_op jit(solution)/shard_map/pallas_call | solution.py:56
  31.4 3.0 %collective-permute-done.f = bf16[4640,128]{1,0:T(8,128)(2,1)S(1)} collective-permute-done((bf16[4640,128]{1,0:T(8,128)(2,1)S(1)}, bf16[4640,128]{1,0:T(8,128)(2,1)S(1)}, u32[]{:S(2)}, u32[]{:S(2)}) %collective-permute-start) | collective-permute-done | bytes 1187872 | tf_op jit(solution)/shard_map/ppermute | solution.py:358
  34.3 2.4 %shard_map.33 = (bf16[2432,128]{1,0:T(8,128)(2,1)S(1)}, bf16[4992,1536]{1,0:T(8,128)(2,1)S(1)}) custom-call(s32[238]{0:T(256)S(1)} %shard_map.28.table, bf16[4640,128]{1,0:T(8,128)(2,1)S(1)} %collective-permute-done.f, bf16[4992,1536]{1,0:T(8,128)(2,1)S(1)} %get-tuple-element.28.left_in), custom_call_target="tpu_custom_call", output_to_operand_aliasing={{1}: (2, {})} | custom-call | bytes 3000000 | tf_op jit(solution)/shard_map/pallas_call | solution.py:56
  36.8 8.2 %collective-permute-done.2.g = bf16[4640,128]{1,0:T(8,128)(2,1)S(1)} collective-permute-done((bf16[4640,128]{1,0:T(8,128)(2,1)S(1)}, bf16[4640,128]{1,0:T(8,128)(2,1)S(1)}, u32[]{:S(2)}, u32[]{:S(2)}) %collective-permute-start.2) | collective-permute-done | bytes 1187872 | tf_op jit(solution)/shard_map/ppermute | solution.py:358
  45.0 0.5 shard_map.34
  45.5 2.1 %collective-permute-start.3 = (bf16[9280,128]{1,0:T(8,128)(2,1)S(1)}, bf16[9280,128]{1,0:T(8,128)(2,1)S(1)}, u32[]{:S(2)}, u32[]{:S(2)}) collective-permute-start(bf16[9280,128]{1,0:T(8,128)(2,1)S(1)} %shard_map.34), channel_id=1, source_target_pairs={{0,1},{1,0},{2,3},{3,2},{4,5},{5,4},{6,7},{7,6},{8,9},{9,8},{10,11... | collective-permute-start | bytes 7127048 | tf_op jit(solution)/shard_map/ppermute | solution.py:358
  47.7 1.9 %collective-permute-start.4 = (bf16[2432,128]{1,0:T(8,128)(2,1)S(1)}, bf16[2432,128]{1,0:T(8,128)(2,1)S(1)}, u32[]{:S(2)}, u32[]{:S(2)}) collective-permute-start(bf16[2432,128]{1,0:T(8,128)(2,1)S(1)} %shard_map.37), channel_id=1, source_target_pairs={{0,511},{1,2},{2,1},{3,4},{4,3},{5,6},{6,5},{7,8},{8,7},{9,10},{10... | collective-permute-start | bytes 1867784 | tf_op jit(solution)/shard_map/ppermute | solution.py:358
  49.6 1.9 %shard_map.35.left_in = bf16[4992,1536]{1,0:T(8,128)(2,1)S(1)} custom-call(s32[238]{0:T(256)S(1)} %shard_map.28.table, bf16[4992,1536]{1,0:T(8,128)(2,1)S(1)} %get-tuple-element.31.left_in, bf16[4640,128]{1,0:T(8,128)(2,1)S(1)} %collective-permute-done.f, bf16[4640,128]{1,0:T(8,128)(2,1)S(1)} %collective-permute-done.2.g), custom_call_target="tpu_custom_call", output_to_operand_aliasing={{}: (1, {})} | custom-call | bytes 12000000 | tf_op jit(solution)/shard_map/pallas_call | solution.py:56
  51.5 0.5 collective-permute-done.3.x
  52.0 7.5 %shard_map.36 = (bf16[4992,1536]{1,0:T(8,128)(2,1)S(1)}, f32[4608,128]{1,0:T(8,128)S(1)}, bf16[4608,128]{1,0:T(8,128)(2,1)}) custom-call(s32[238]{0:T(256)S(1)} %shard_map.28.table, bf16[4992,1536]{1,0:T(8,128)(2,1)S(1)} %shard_map.35.left_in, f32[4608,128]{1,0:T(8,128)S(1)} %get-tuple-element.33.total_in, ...), custom_call_target="tpu_custom_call", output_to_operand_aliasing={{0}: (1, {}), {1}: (2, {})} | custom-call | bytes 12000000 | tf_op jit(solution)/shard_map/pallas_call | solution.py:56
  59.5 0.1 collective-permute-done.4.relay
  59.5 5.0 %shard_map.38 = (bf16[4992,1536]{1,0:T(8,128)(2,1)S(1)}, f32[4608,128]{1,0:T(8,128)S(1)}, bf16[4608,128]{1,0:T(8,128)(2,1)}) custom-call(s32[238]{0:T(256)S(1)} %shard_map.28.table, bf16[4992,1536]{1,0:T(8,128)(2,1)S(1)} %get-tuple-element.35.left_in, ...), custom_call_target="tpu_custom_call", output_to_operand_aliasing={{0}: (1, {}), {1}: (2, {}), {2}: (5, {})} | custom-call | bytes 12000000 | tf_op jit(solution)/shard_map/pallas_call | solution.py:56
  (1 shorter events, 0.0 us)
Async XLA Ops:
  0.0 23.0 %copy-start = (s32[3,12]{1,0:T(4,128)S(1)}, s32[3,12]{1,0:T(4,128)}, u32[]{:S(2)}) copy-start(s32[3,12]{1,0:T(4,128)} %rows.3) | copy-start | bytes 436
  1.3 33.0 %collective-permute-start = (bf16[4640,128]{1,0:T(8,128)(2,1)S(1)}, bf16[4640,128]{1,0:T(8,128)(2,1)S(1)}, u32[]{:S(2)}, u32[]{:S(2)}) collective-permute-start(bf16[4640,128]{1,0:T(8,128)(2,1)S(1)} %shard_map.29.longer), channel_id=1, source_target_pairs={{0,510},{1,3},{2,0},{3,5},{4,2},{5,7},{6,4},{7,9},{8,6},{9,11},{10... | collective-permute-start | bytes 3563528 | tf_op jit(solution)/shard_map/ppermute | solution.py:358
  5.4 39.6 %collective-permute-start.2 = (bf16[4640,128]{1,0:T(8,128)(2,1)S(1)}, bf16[4640,128]{1,0:T(8,128)(2,1)S(1)}, u32[]{:S(2)}, u32[]{:S(2)}) collective-permute-start(bf16[4640,128]{1,0:T(8,128)(2,1)S(1)} %shard_map.29.longer), channel_id=1, source_target_pairs={{0,2},{1,511},{2,4},{3,1},{4,6},{5,3},{6,8},{7,5},{8,10},{9,7},{10... | collective-permute-start | bytes 3563528 | tf_op jit(solution)/shard_map/ppermute | solution.py:358
  20.1 8.1 %collective-permute-start.1 = (bf16[4624,128]{1,0:T(8,128)(2,1)S(1)}, bf16[4624,128]{1,0:T(8,128)(2,1)S(1)}, u32[]{:S(2)}, u32[]{:S(2)}) collective-permute-start(bf16[4624,128]{1,0:T(8,128)(2,1)S(1)} %shard_map.30.mine), channel_id=1, source_target_pairs={{0,1},{1,0},{2,3},{3,2},{4,5},{5,4},{6,7},{7,6},{8,9},{9,8},{10,11... | collective-permute-start | bytes 3551240 | tf_op jit(solution)/shard_map/ppermute | solution.py:358
  45.5 6.5 %collective-permute-start.3 = (bf16[9280,128]{1,0:T(8,128)(2,1)S(1)}, bf16[9280,128]{1,0:T(8,128)(2,1)S(1)}, u32[]{:S(2)}, u32[]{:S(2)}) collective-permute-start(bf16[9280,128]{1,0:T(8,128)(2,1)S(1)} %shard_map.34), channel_id=1, source_target_pairs={{0,1},{1,0},{2,3},{3,2},{4,5},{5,4},{6,7},{7,6},{8,9},{9,8},{10,11... | collective-permute-start | bytes 7127048 | tf_op jit(solution)/shard_map/ppermute | solution.py:358
  47.7 11.8 %collective-permute-start.4 = (bf16[2432,128]{1,0:T(8,128)(2,1)S(1)}, bf16[2432,128]{1,0:T(8,128)(2,1)S(1)}, u32[]{:S(2)}, u32[]{:S(2)}) collective-permute-start(bf16[2432,128]{1,0:T(8,128)(2,1)S(1)} %shard_map.37), channel_id=1, source_target_pairs={{0,511},{1,2},{2,1},{3,4},{4,3},{5,6},{6,5},{7,8},{8,7},{9,10},{10... | collective-permute-start | bytes 1867784 | tf_op jit(solution)/shard_map/ppermute | solution.py:358

commit v5 on v4

--- a/solution.py
+++ b/solution.py
@@ -50,7 +50,9 @@
 
 def call(kernel, out_shape, in_specs, out_specs, scratch, aliases, micros, *args):
     args = [
-        pltpu.with_memory_space_constraint(arg, spec.memory_space) if spec in (VMEM, HBM) else arg
+        pltpu.with_memory_space_constraint(arg, spec.memory_space)
+        if spec in (VMEM, HBM) or arg.shape == (TABLE,)
+        else arg
         for arg, spec in zip(args, in_specs)
     ]
     return pl.pallas_call(
@@ -412,7 +414,7 @@
     g = send(longer, inward)
     table = call(
         functools.partial(table_kernel, columns),
-        jax.ShapeDtypeStruct((TABLE,), jnp.int32),
+        pltpu.SMEM((TABLE,), jnp.int32),
         [SMEM, SMEM],
         SMEM,
         [],

time: 65.6 us -> 64.1 us (0.977)
  Pallas kernels: 27.3 us -> 24.1 us
  waiting for transfers between devices: 11.7 us -> 14.2 us
    pallas_call x11, Pallas kernels: 27.3 us -> 24.1 us  [call(): pl.pallas_call(kernel, out_shape=out_shape, in_specs=in_specs, out_specs=...]
    ppermute x5, waiting for transfers between devices: 11.7 us -> 14.2 us  [send(): return lax.ppermute(value, AXES, pairs)]
  transfers between devices with their start and end apart: 5 -> 5, of which waited for: 4 -> 4; matrix products, arithmetic and copies ran while one was open for 0% -> 0% of each run, Pallas kernels for 32% -> 28%
where the time goes in v5:
time: 64.1 us; the launch traced here: 63.8 us
  starting transfers between devices  25.2 us (39%)
  Pallas kernels  24.1 us (38%)
  waiting for transfers between devices  14.2 us (22%)
    ppermute x5, starting transfers between devices, send(): return lax.ppermute(value, AXES, pairs)  25.2 us
    pallas_call x11, Pallas kernels, call(): pl.pallas_call(kernel, out_shape=out_shape, in_specs=in_specs, out_specs=...  24.1 us
    ppermute x5, waiting for transfers between devices, send(): return lax.ppermute(value, AXES, pairs)  14.2 us
  transfers between devices with their start and end apart: 5, of which 4 were waited for; matrix products, arithmetic and copies ran while one was open for 0% of the time, Pallas kernels for 28%

profile of v5, /device:TPU:1, one launch (start us, length us, event | category | flops | bytes accessed | tf_op | source)
XLA Modules:
  0.0 63.8 jit_solution(1583088671512798934)
XLA Ops:
  0.0 0.0 copy-start
  0.0 1.3 %shard_map.29.longer = bf16[4640,128]{1,0:T(8,128)(2,1)S(1)} custom-call(s32[1]{0:T(128)} %bitcast.device, s32[3,12]{1,0:T(4,128)} %rows.3, bf16[4608,128]{1,0:T(8,128)(2,1)} %bitcast.3), custom_call_target="tpu_custom_call" | custom-call | bytes 3000000 | tf_op jit(solution)/shard_map/pallas_call | solution.py:58
  1.3 4.0 %collective-permute-start = (bf16[4640,128]{1,0:T(8,128)(2,1)S(1)}, bf16[4640,128]{1,0:T(8,128)(2,1)S(1)}, u32[]{:S(2)}, u32[]{:S(2)}) collective-permute-start(bf16[4640,128]{1,0:T(8,128)(2,1)S(1)} %shard_map.29.longer), channel_id=1, source_target_pairs={{0,510},{1,3},{2,0},{3,5},{4,2},{5,7},{6,4},{7,9},{8,6},{9,11},{10... | collective-permute-start | bytes 3563528 | tf_op jit(solution)/shard_map/ppermute | solution.py:360
  5.4 14.5 %collective-permute-start.2 = (bf16[4640,128]{1,0:T(8,128)(2,1)S(1)}, bf16[4640,128]{1,0:T(8,128)(2,1)S(1)}, u32[]{:S(2)}, u32[]{:S(2)}) collective-permute-start(bf16[4640,128]{1,0:T(8,128)(2,1)S(1)} %shard_map.29.longer), channel_id=1, source_target_pairs={{0,2},{1,511},{2,4},{3,1},{4,6},{5,3},{6,8},{7,5},{8,10},{9,7},{10... | collective-permute-start | bytes 3563528 | tf_op jit(solution)/shard_map/ppermute | solution.py:360
  19.8 0.3 shard_map.30.mine
  20.1 2.9 %collective-permute-start.1 = (bf16[4624,128]{1,0:T(8,128)(2,1)S(1)}, bf16[4624,128]{1,0:T(8,128)(2,1)S(1)}, u32[]{:S(2)}, u32[]{:S(2)}) collective-permute-start(bf16[4624,128]{1,0:T(8,128)(2,1)S(1)} %shard_map.30.mine), channel_id=1, source_target_pairs={{0,1},{1,0},{2,3},{3,2},{4,5},{5,4},{6,7},{7,6},{8,9},{9,8},{10,11... | collective-permute-start | bytes 3551240 | tf_op jit(solution)/shard_map/ppermute | solution.py:360
  23.0 0.0 copy-done
  23.0 1.7 %shard_map.28.table = s32[238]{0:T(256)S(4)} custom-call(s32[1]{0:T(128)} %bitcast.device, s32[3,12]{1,0:T(4,128)S(1)} %copy-done), custom_call_target="tpu_custom_call" | custom-call | bytes 6000000 | tf_op jit(solution)/shard_map/pallas_call | solution.py:58
  24.7 2.6 %shard_map.31 = (bf16[4992,1536]{1,0:T(8,128)(2,1)S(1)}, f32[4608,128]{1,0:T(8,128)S(1)}, bf16[4608,128]{1,0:T(8,128)(2,1)S(1)}) custom-call(s32[238]{0:T(256)S(4)} %shard_map.28.table, bf16[4624,128]{1,0:T(8,128)(2,1)S(1)} %shard_map.30.mine), custom_call_target="tpu_custom_call" | custom-call | bytes 24000000 | tf_op jit(solution)/shard_map/pallas_call | solution.py:58
  27.3 0.0 collective-permute-done.1.refs_0_
  27.3 4.0 %shard_map.32 = (bf16[4992,1536]{1,0:T(8,128)(2,1)S(1)}, f32[4608,128]{1,0:T(8,128)S(1)}) custom-call(s32[238]{0:T(256)S(4)} %shard_map.28.table, bf16[4992,1536]{1,0:T(8,128)(2,1)S(1)} %get-tuple-element.23.left_in, f32[4608,128]{1,0:T(8,128)S(1)} %get-tuple-element.24.total_in, ...), custom_call_target="tpu_custom_call", output_to_operand_aliasing={{0}: (1, {}), {1}: (2, {})} | custom-call | bytes 12000000 | tf_op jit(solution)/shard_map/pallas_call | solution.py:58
  31.3 3.1 %collective-permute-done.f = bf16[4640,128]{1,0:T(8,128)(2,1)S(1)} collective-permute-done((bf16[4640,128]{1,0:T(8,128)(2,1)S(1)}, bf16[4640,128]{1,0:T(8,128)(2,1)S(1)}, u32[]{:S(2)}, u32[]{:S(2)}) %collective-permute-start) | collective-permute-done | bytes 1187872 | tf_op jit(solution)/shard_map/ppermute | solution.py:360
  34.3 1.7 %shard_map.33 = (bf16[2432,128]{1,0:T(8,128)(2,1)S(1)}, bf16[4992,1536]{1,0:T(8,128)(2,1)S(1)}) custom-call(s32[238]{0:T(256)S(4)} %shard_map.28.table, bf16[4640,128]{1,0:T(8,128)(2,1)S(1)} %collective-permute-done.f, bf16[4992,1536]{1,0:T(8,128)(2,1)S(1)} %get-tuple-element.28.left_in), custom_call_target="tpu_custom_call", output_to_operand_aliasing={{1}: (2, {})} | custom-call | bytes 3000000 | tf_op jit(solution)/shard_map/pallas_call | solution.py:58
  36.1 8.9 %collective-permute-done.2.g = bf16[4640,128]{1,0:T(8,128)(2,1)S(1)} collective-permute-done((bf16[4640,128]{1,0:T(8,128)(2,1)S(1)}, bf16[4640,128]{1,0:T(8,128)(2,1)S(1)}, u32[]{:S(2)}, u32[]{:S(2)}) %collective-permute-start.2) | collective-permute-done | bytes 1187872 | tf_op jit(solution)/shard_map/ppermute | solution.py:360
  45.0 0.5 shard_map.34
  45.5 1.9 %collective-permute-start.3 = (bf16[9280,128]{1,0:T(8,128)(2,1)S(1)}, bf16[9280,128]{1,0:T(8,128)(2,1)S(1)}, u32[]{:S(2)}, u32[]{:S(2)}) collective-permute-start(bf16[9280,128]{1,0:T(8,128)(2,1)S(1)} %shard_map.34), channel_id=1, source_target_pairs={{0,1},{1,0},{2,3},{3,2},{4,5},{5,4},{6,7},{7,6},{8,9},{9,8},{10,11... | collective-permute-start | bytes 7127048 | tf_op jit(solution)/shard_map/ppermute | solution.py:360
  47.5 1.9 %collective-permute-start.4 = (bf16[2432,128]{1,0:T(8,128)(2,1)S(1)}, bf16[2432,128]{1,0:T(8,128)(2,1)S(1)}, u32[]{:S(2)}, u32[]{:S(2)}) collective-permute-start(bf16[2432,128]{1,0:T(8,128)(2,1)S(1)} %shard_map.37), channel_id=1, source_target_pairs={{0,511},{1,2},{2,1},{3,4},{4,3},{5,6},{6,5},{7,8},{8,7},{9,10},{10... | collective-permute-start | bytes 1867784 | tf_op jit(solution)/shard_map/ppermute | solution.py:360
  49.4 1.6 %shard_map.35.left_in = bf16[4992,1536]{1,0:T(8,128)(2,1)S(1)} custom-call(s32[238]{0:T(256)S(4)} %shard_map.28.table, bf16[4992,1536]{1,0:T(8,128)(2,1)S(1)} %get-tuple-element.31.left_in, bf16[4640,128]{1,0:T(8,128)(2,1)S(1)} %collective-permute-done.f, bf16[4640,128]{1,0:T(8,128)(2,1)S(1)} %collective-permute-done.2.g), custom_call_target="tpu_custom_call", output_to_operand_aliasing={{}: (1, {})} | custom-call | bytes 12000000 | tf_op jit(solution)/shard_map/pallas_call | solution.py:58
  51.0 0.9 %collective-permute-done.3.x = bf16[9280,128]{1,0:T(8,128)(2,1)S(1)} collective-permute-done((bf16[9280,128]{1,0:T(8,128)(2,1)S(1)}, bf16[9280,128]{1,0:T(8,128)(2,1)S(1)}, u32[]{:S(2)}, u32[]{:S(2)}) %collective-permute-start.3) | collective-permute-done | bytes 2375712 | tf_op jit(solution)/shard_map/ppermute | solution.py:360
  52.0 6.1 %shard_map.36 = (bf16[4992,1536]{1,0:T(8,128)(2,1)S(1)}, f32[4608,128]{1,0:T(8,128)S(1)}, bf16[4608,128]{1,0:T(8,128)(2,1)}) custom-call(s32[238]{0:T(256)S(4)} %shard_map.28.table, bf16[4992,1536]{1,0:T(8,128)(2,1)S(1)} %shard_map.35.left_in, f32[4608,128]{1,0:T(8,128)S(1)} %get-tuple-element.33.total_in, ...), custom_call_target="tpu_custom_call", output_to_operand_aliasing={{0}: (1, {}), {1}: (2, {})} | custom-call | bytes 12000000 | tf_op jit(solution)/shard_map/pallas_call | solution.py:58
  58.1 1.2 %collective-permute-done.4.relay = bf16[2432,128]{1,0:T(8,128)(2,1)S(1)} collective-permute-done((bf16[2432,128]{1,0:T(8,128)(2,1)S(1)}, bf16[2432,128]{1,0:T(8,128)(2,1)S(1)}, u32[]{:S(2)}, u32[]{:S(2)}) %collective-permute-start.4) | collective-permute-done | bytes 622624 | tf_op jit(solution)/shard_map/ppermute | solution.py:360
  59.3 4.3 %shard_map.38 = (bf16[4992,1536]{1,0:T(8,128)(2,1)S(1)}, f32[4608,128]{1,0:T(8,128)S(1)}, bf16[4608,128]{1,0:T(8,128)(2,1)}) custom-call(s32[238]{0:T(256)S(4)} %shard_map.28.table, bf16[4992,1536]{1,0:T(8,128)(2,1)S(1)} %get-tuple-element.35.left_in, ...), custom_call_target="tpu_custom_call", output_to_operand_aliasing={{0}: (1, {}), {1}: (2, {}), {2}: (5, {})} | custom-call | bytes 12000000 | tf_op jit(solution)/shard_map/pallas_call | solution.py:58
  (1 shorter events, 0.0 us)
Async XLA Ops:
  0.0 23.0 %copy-start = (s32[3,12]{1,0:T(4,128)S(1)}, s32[3,12]{1,0:T(4,128)}, u32[]{:S(2)}) copy-start(s32[3,12]{1,0:T(4,128)} %rows.3) | copy-start | bytes 436
  1.3 33.0 %collective-permute-start = (bf16[4640,128]{1,0:T(8,128)(2,1)S(1)}, bf16[4640,128]{1,0:T(8,128)(2,1)S(1)}, u32[]{:S(2)}, u32[]{:S(2)}) collective-permute-start(bf16[4640,128]{1,0:T(8,128)(2,1)S(1)} %shard_map.29.longer), channel_id=1, source_target_pairs={{0,510},{1,3},{2,0},{3,5},{4,2},{5,7},{6,4},{7,9},{8,6},{9,11},{10... | collective-permute-start | bytes 3563528 | tf_op jit(solution)/shard_map/ppermute | solution.py:360
  5.4 39.6 %collective-permute-start.2 = (bf16[4640,128]{1,0:T(8,128)(2,1)S(1)}, bf16[4640,128]{1,0:T(8,128)(2,1)S(1)}, u32[]{:S(2)}, u32[]{:S(2)}) collective-permute-start(bf16[4640,128]{1,0:T(8,128)(2,1)S(1)} %shard_map.29.longer), channel_id=1, source_target_pairs={{0,2},{1,511},{2,4},{3,1},{4,6},{5,3},{6,8},{7,5},{8,10},{9,7},{10... | collective-permute-start | bytes 3563528 | tf_op jit(solution)/shard_map/ppermute | solution.py:360
  20.1 7.2 %collective-permute-start.1 = (bf16[4624,128]{1,0:T(8,128)(2,1)S(1)}, bf16[4624,128]{1,0:T(8,128)(2,1)S(1)}, u32[]{:S(2)}, u32[]{:S(2)}) collective-permute-start(bf16[4624,128]{1,0:T(8,128)(2,1)S(1)} %shard_map.30.mine), channel_id=1, source_target_pairs={{0,1},{1,0},{2,3},{3,2},{4,5},{5,4},{6,7},{7,6},{8,9},{9,8},{10,11... | collective-permute-start | bytes 3551240 | tf_op jit(solution)/shard_map/ppermute | solution.py:360
  45.5 6.5 %collective-permute-start.3 = (bf16[9280,128]{1,0:T(8,128)(2,1)S(1)}, bf16[9280,128]{1,0:T(8,128)(2,1)S(1)}, u32[]{:S(2)}, u32[]{:S(2)}) collective-permute-start(bf16[9280,128]{1,0:T(8,128)(2,1)S(1)} %shard_map.34), channel_id=1, source_target_pairs={{0,1},{1,0},{2,3},{3,2},{4,5},{5,4},{6,7},{7,6},{8,9},{9,8},{10,11... | collective-permute-start | bytes 7127048 | tf_op jit(solution)/shard_map/ppermute | solution.py:360
  47.5 11.8 %collective-permute-start.4 = (bf16[2432,128]{1,0:T(8,128)(2,1)S(1)}, bf16[2432,128]{1,0:T(8,128)(2,1)S(1)}, u32[]{:S(2)}, u32[]{:S(2)}) collective-permute-start(bf16[2432,128]{1,0:T(8,128)(2,1)S(1)} %shard_map.37), channel_id=1, source_target_pairs={{0,511},{1,2},{2,1},{3,4},{4,3},{5,6},{6,5},{7,8},{8,7},{9,10},{10... | collective-permute-start | bytes 1867784 | tf_op jit(solution)/shard_map/ppermute | solution.py:360

commit v6 on v5

--- a/solution.py
+++ b/solution.py
@@ -75,17 +75,26 @@
 
 
 def pack_kernel(total, device, rows, mine, longer, near_rows, wide, sem):
-    body = pltpu.make_async_copy(mine, longer.at[pl.ds(0, BODY)], sem.at[0])
-    lists = pltpu.make_async_copy(rows, near_rows, sem.at[1])
-    body.start()
+    lists = pltpu.make_async_copy(rows, near_rows, sem.at[0])
     lists.start()
+    pieces = [
+        pltpu.make_async_copy(
+            mine.at[pl.ds(i * BODY // 4, BODY // 4)],
+            longer.at[pl.ds(i * BODY // 4, BODY // 4)],
+            sem.at[1 + i],
+        )
+        for i in range(4)
+    ]
+    for piece in pieces:
+        piece.start()
     column = device[0] * COLS + lax.broadcasted_iota(jnp.int32, (COLS, SLOTS), 0)
     wide[...] = jnp.zeros_like(wide)
     longer[pl.ds(FULL, META), :] = jnp.zeros((META, TILE), BF16)
     lists.wait()
     wide[pl.ds(0, COLS), pl.ds(0, SLOTS)] = wrapped(near_rows[...] - column, total).astype(F32)
     longer[pl.ds(BODY, META), :] = wide[...].astype(BF16)
-    body.wait()
+    for piece in pieces:
+        piece.wait()
 
 
 def shorten_kernel(longer, packed, sem):
@@ -291,7 +300,6 @@
 
 
 def fill_relay(odd, f, relay, offsets):
-    relay[...] = jnp.zeros_like(relay)
     for column, start, size, shift in (
         (1, 0, FAR, 0 if odd else BAND),
         (2 * odd, FAR, NEAR, 1 if odd else BAND),
@@ -316,7 +324,9 @@
 
     @pl.when(table[ODD_AT] == 1)
     def _():
-        read_meta(f, whole, offsets, sem).wait()
+        copy = read_meta(f, whole, offsets, sem)
+        relay[...] = jnp.zeros_like(relay)
+        copy.wait()
         fill_relay(1, f, relay, offsets)
         scatter(table, left, f, -6, lambda j, p: offsets[j, p])
 
@@ -326,7 +336,9 @@
 
     @pl.when(device[0] % 2 == 0)
     def _():
-        read_meta(f, whole, offsets, sem).wait()
+        copy = read_meta(f, whole, offsets, sem)
+        relay[...] = jnp.zeros_like(relay)
+        copy.wait()
         fill_relay(0, f, relay, offsets)
 
 
@@ -391,7 +403,7 @@
         [
             pltpu.VMEM((COLS, SLOTS), jnp.int32),
             pltpu.VMEM((META, TILE), F32),
-            pltpu.SemaphoreType.DMA((2,)),
+            pltpu.SemaphoreType.DMA((5,)),
         ],
         {},
         1,

time: 64.1 us -> 64.1 us (level)
  no operation moved by 1% of the time
where the time goes in v6:
time: 64.1 us; the launch traced here: 63.8 us
  starting transfers between devices  25.2 us (39%)
  Pallas kernels  23.8 us (37%)
  waiting for transfers between devices  14.5 us (23%)
    ppermute x5, starting transfers between devices, send(): return lax.ppermute(value, AXES, pairs)  25.2 us
    pallas_call x11, Pallas kernels, call(): pl.pallas_call(kernel, out_shape=out_shape, in_specs=in_specs, out_specs=...  23.8 us
    ppermute x5, waiting for transfers between devices, send(): return lax.ppermute(value, AXES, pairs)  14.5 us
  transfers between devices with their start and end apart: 5, of which 4 were waited for; matrix products, arithmetic and copies ran while one was open for 0% of the time, Pallas kernels for 28%

profile of v6, /device:TPU:1, one launch (start us, length us, event | category | flops | bytes accessed | tf_op | source)
XLA Modules:
  0.0 63.8 jit_solution(10939620187327397235)
XLA Ops:
  0.0 0.0 copy-start
  0.0 1.3 %shard_map.29.longer = bf16[4640,128]{1,0:T(8,128)(2,1)S(1)} custom-call(s32[1]{0:T(128)} %bitcast.device, s32[3,12]{1,0:T(4,128)} %rows.3, bf16[4608,128]{1,0:T(8,128)(2,1)} %bitcast.3), custom_call_target="tpu_custom_call" | custom-call | bytes 3000000 | tf_op jit(solution)/shard_map/pallas_call | solution.py:58
  1.3 4.0 %collective-permute-start = (bf16[4640,128]{1,0:T(8,128)(2,1)S(1)}, bf16[4640,128]{1,0:T(8,128)(2,1)S(1)}, u32[]{:S(2)}, u32[]{:S(2)}) collective-permute-start(bf16[4640,128]{1,0:T(8,128)(2,1)S(1)} %shard_map.29.longer), channel_id=1, source_target_pairs={{0,510},{1,3},{2,0},{3,5},{4,2},{5,7},{6,4},{7,9},{8,6},{9,11},{10... | collective-permute-start | bytes 3563528 | tf_op jit(solution)/shard_map/ppermute | solution.py:372
  5.4 14.5 %collective-permute-start.2 = (bf16[4640,128]{1,0:T(8,128)(2,1)S(1)}, bf16[4640,128]{1,0:T(8,128)(2,1)S(1)}, u32[]{:S(2)}, u32[]{:S(2)}) collective-permute-start(bf16[4640,128]{1,0:T(8,128)(2,1)S(1)} %shard_map.29.longer), channel_id=1, source_target_pairs={{0,2},{1,511},{2,4},{3,1},{4,6},{5,3},{6,8},{7,5},{8,10},{9,7},{10... | collective-permute-start | bytes 3563528 | tf_op jit(solution)/shard_map/ppermute | solution.py:372
  19.8 0.3 shard_map.30.mine
  20.1 2.9 %collective-permute-start.1 = (bf16[4624,128]{1,0:T(8,128)(2,1)S(1)}, bf16[4624,128]{1,0:T(8,128)(2,1)S(1)}, u32[]{:S(2)}, u32[]{:S(2)}) collective-permute-start(bf16[4624,128]{1,0:T(8,128)(2,1)S(1)} %shard_map.30.mine), channel_id=1, source_target_pairs={{0,1},{1,0},{2,3},{3,2},{4,5},{5,4},{6,7},{7,6},{8,9},{9,8},{10,11... | collective-permute-start | bytes 3551240 | tf_op jit(solution)/shard_map/ppermute | solution.py:372
  23.0 0.0 copy-done
  23.0 1.7 %shard_map.28.table = s32[238]{0:T(256)S(4)} custom-call(s32[1]{0:T(128)} %bitcast.device, s32[3,12]{1,0:T(4,128)S(1)} %copy-done), custom_call_target="tpu_custom_call" | custom-call | bytes 6000000 | tf_op jit(solution)/shard_map/pallas_call | solution.py:58
  24.7 2.6 %shard_map.31 = (bf16[4992,1536]{1,0:T(8,128)(2,1)S(1)}, f32[4608,128]{1,0:T(8,128)S(1)}, bf16[4608,128]{1,0:T(8,128)(2,1)S(1)}) custom-call(s32[238]{0:T(256)S(4)} %shard_map.28.table, bf16[4624,128]{1,0:T(8,128)(2,1)S(1)} %shard_map.30.mine), custom_call_target="tpu_custom_call" | custom-call | bytes 24000000 | tf_op jit(solution)/shard_map/pallas_call | solution.py:58
  27.3 0.0 collective-permute-done.1.refs_0_
  27.3 3.5 %shard_map.32 = (bf16[4992,1536]{1,0:T(8,128)(2,1)S(1)}, f32[4608,128]{1,0:T(8,128)S(1)}) custom-call(s32[238]{0:T(256)S(4)} %shard_map.28.table, bf16[4992,1536]{1,0:T(8,128)(2,1)S(1)} %get-tuple-element.23.left_in, f32[4608,128]{1,0:T(8,128)S(1)} %get-tuple-element.24.total_in, ...), custom_call_target="tpu_custom_call", output_to_operand_aliasing={{0}: (1, {}), {1}: (2, {})} | custom-call | bytes 12000000 | tf_op jit(solution)/shard_map/pallas_call | solution.py:58
  30.9 3.4 %collective-permute-done.f = bf16[4640,128]{1,0:T(8,128)(2,1)S(1)} collective-permute-done((bf16[4640,128]{1,0:T(8,128)(2,1)S(1)}, bf16[4640,128]{1,0:T(8,128)(2,1)S(1)}, u32[]{:S(2)}, u32[]{:S(2)}) %collective-permute-start) | collective-permute-done | bytes 1187872 | tf_op jit(solution)/shard_map/ppermute | solution.py:372
  34.3 1.9 %shard_map.33 = (bf16[2432,128]{1,0:T(8,128)(2,1)S(1)}, bf16[4992,1536]{1,0:T(8,128)(2,1)S(1)}) custom-call(s32[238]{0:T(256)S(4)} %shard_map.28.table, bf16[4640,128]{1,0:T(8,128)(2,1)S(1)} %collective-permute-done.f, bf16[4992,1536]{1,0:T(8,128)(2,1)S(1)} %get-tuple-element.28.left_in), custom_call_target="tpu_custom_call", output_to_operand_aliasing={{1}: (2, {})} | custom-call | bytes 3000000 | tf_op jit(solution)/shard_map/pallas_call | solution.py:58
  36.2 8.8 %collective-permute-done.2.g = bf16[4640,128]{1,0:T(8,128)(2,1)S(1)} collective-permute-done((bf16[4640,128]{1,0:T(8,128)(2,1)S(1)}, bf16[4640,128]{1,0:T(8,128)(2,1)S(1)}, u32[]{:S(2)}, u32[]{:S(2)}) %collective-permute-start.2) | collective-permute-done | bytes 1187872 | tf_op jit(solution)/shard_map/ppermute | solution.py:372
  45.0 0.5 shard_map.34
  45.5 1.9 %collective-permute-start.3 = (bf16[9280,128]{1,0:T(8,128)(2,1)S(1)}, bf16[9280,128]{1,0:T(8,128)(2,1)S(1)}, u32[]{:S(2)}, u32[]{:S(2)}) collective-permute-start(bf16[9280,128]{1,0:T(8,128)(2,1)S(1)} %shard_map.34), channel_id=1, source_target_pairs={{0,1},{1,0},{2,3},{3,2},{4,5},{5,4},{6,7},{7,6},{8,9},{9,8},{10,11... | collective-permute-start | bytes 7127048 | tf_op jit(solution)/shard_map/ppermute | solution.py:372
  47.5 1.9 %collective-permute-start.4 = (bf16[2432,128]{1,0:T(8,128)(2,1)S(1)}, bf16[2432,128]{1,0:T(8,128)(2,1)S(1)}, u32[]{:S(2)}, u32[]{:S(2)}) collective-permute-start(bf16[2432,128]{1,0:T(8,128)(2,1)S(1)} %shard_map.37), channel_id=1, source_target_pairs={{0,511},{1,2},{2,1},{3,4},{4,3},{5,6},{6,5},{7,8},{8,7},{9,10},{10... | collective-permute-start | bytes 1867784 | tf_op jit(solution)/shard_map/ppermute | solution.py:372
  49.4 1.5 %shard_map.35.left_in = bf16[4992,1536]{1,0:T(8,128)(2,1)S(1)} custom-call(s32[238]{0:T(256)S(4)} %shard_map.28.table, bf16[4992,1536]{1,0:T(8,128)(2,1)S(1)} %get-tuple-element.31.left_in, bf16[4640,128]{1,0:T(8,128)(2,1)S(1)} %collective-permute-done.f, bf16[4640,128]{1,0:T(8,128)(2,1)S(1)} %collective-permute-done.2.g), custom_call_target="tpu_custom_call", output_to_operand_aliasing={{}: (1, {})} | custom-call | bytes 12000000 | tf_op jit(solution)/shard_map/pallas_call | solution.py:58
  50.9 1.0 %collective-permute-done.3.x = bf16[9280,128]{1,0:T(8,128)(2,1)S(1)} collective-permute-done((bf16[9280,128]{1,0:T(8,128)(2,1)S(1)}, bf16[9280,128]{1,0:T(8,128)(2,1)S(1)}, u32[]{:S(2)}, u32[]{:S(2)}) %collective-permute-start.3) | collective-permute-done | bytes 2375712 | tf_op jit(solution)/shard_map/ppermute | solution.py:372
  52.0 6.1 %shard_map.36 = (bf16[4992,1536]{1,0:T(8,128)(2,1)S(1)}, f32[4608,128]{1,0:T(8,128)S(1)}, bf16[4608,128]{1,0:T(8,128)(2,1)}) custom-call(s32[238]{0:T(256)S(4)} %shard_map.28.table, bf16[4992,1536]{1,0:T(8,128)(2,1)S(1)} %shard_map.35.left_in, f32[4608,128]{1,0:T(8,128)S(1)} %get-tuple-element.33.total_in, ...), custom_call_target="tpu_custom_call", output_to_operand_aliasing={{0}: (1, {}), {1}: (2, {})} | custom-call | bytes 12000000 | tf_op jit(solution)/shard_map/pallas_call | solution.py:58
  58.1 1.2 %collective-permute-done.4.relay = bf16[2432,128]{1,0:T(8,128)(2,1)S(1)} collective-permute-done((bf16[2432,128]{1,0:T(8,128)(2,1)S(1)}, bf16[2432,128]{1,0:T(8,128)(2,1)S(1)}, u32[]{:S(2)}, u32[]{:S(2)}) %collective-permute-start.4) | collective-permute-done | bytes 622624 | tf_op jit(solution)/shard_map/ppermute | solution.py:372
  59.3 4.3 %shard_map.38 = (bf16[4992,1536]{1,0:T(8,128)(2,1)S(1)}, f32[4608,128]{1,0:T(8,128)S(1)}, bf16[4608,128]{1,0:T(8,128)(2,1)}) custom-call(s32[238]{0:T(256)S(4)} %shard_map.28.table, bf16[4992,1536]{1,0:T(8,128)(2,1)S(1)} %get-tuple-element.35.left_in, ...), custom_call_target="tpu_custom_call", output_to_operand_aliasing={{0}: (1, {}), {1}: (2, {}), {2}: (5, {})} | custom-call | bytes 12000000 | tf_op jit(solution)/shard_map/pallas_call | solution.py:58
  (1 shorter events, 0.0 us)
Async XLA Ops:
  0.0 23.0 %copy-start = (s32[3,12]{1,0:T(4,128)S(1)}, s32[3,12]{1,0:T(4,128)}, u32[]{:S(2)}) copy-start(s32[3,12]{1,0:T(4,128)} %rows.3) | copy-start | bytes 436
  1.3 33.0 %collective-permute-start = (bf16[4640,128]{1,0:T(8,128)(2,1)S(1)}, bf16[4640,128]{1,0:T(8,128)(2,1)S(1)}, u32[]{:S(2)}, u32[]{:S(2)}) collective-permute-start(bf16[4640,128]{1,0:T(8,128)(2,1)S(1)} %shard_map.29.longer), channel_id=1, source_target_pairs={{0,510},{1,3},{2,0},{3,5},{4,2},{5,7},{6,4},{7,9},{8,6},{9,11},{10... | collective-permute-start | bytes 3563528 | tf_op jit(solution)/shard_map/ppermute | solution.py:372
  5.4 39.6 %collective-permute-start.2 = (bf16[4640,128]{1,0:T(8,128)(2,1)S(1)}, bf16[4640,128]{1,0:T(8,128)(2,1)S(1)}, u32[]{:S(2)}, u32[]{:S(2)}) collective-permute-start(bf16[4640,128]{1,0:T(8,128)(2,1)S(1)} %shard_map.29.longer), channel_id=1, source_target_pairs={{0,2},{1,511},{2,4},{3,1},{4,6},{5,3},{6,8},{7,5},{8,10},{9,7},{10... | collective-permute-start | bytes 3563528 | tf_op jit(solution)/shard_map/ppermute | solution.py:372
  20.1 7.2 %collective-permute-start.1 = (bf16[4624,128]{1,0:T(8,128)(2,1)S(1)}, bf16[4624,128]{1,0:T(8,128)(2,1)S(1)}, u32[]{:S(2)}, u32[]{:S(2)}) collective-permute-start(bf16[4624,128]{1,0:T(8,128)(2,1)S(1)} %shard_map.30.mine), channel_id=1, source_target_pairs={{0,1},{1,0},{2,3},{3,2},{4,5},{5,4},{6,7},{7,6},{8,9},{9,8},{10,11... | collective-permute-start | bytes 3551240 | tf_op jit(solution)/shard_map/ppermute | solution.py:372
  45.5 6.5 %collective-permute-start.3 = (bf16[9280,128]{1,0:T(8,128)(2,1)S(1)}, bf16[9280,128]{1,0:T(8,128)(2,1)S(1)}, u32[]{:S(2)}, u32[]{:S(2)}) collective-permute-start(bf16[9280,128]{1,0:T(8,128)(2,1)S(1)} %shard_map.34), channel_id=1, source_target_pairs={{0,1},{1,0},{2,3},{3,2},{4,5},{5,4},{6,7},{7,6},{8,9},{9,8},{10,11... | collective-permute-start | bytes 7127048 | tf_op jit(solution)/shard_map/ppermute | solution.py:372
  47.5 11.8 %collective-permute-start.4 = (bf16[2432,128]{1,0:T(8,128)(2,1)S(1)}, bf16[2432,128]{1,0:T(8,128)(2,1)S(1)}, u32[]{:S(2)}, u32[]{:S(2)}) collective-permute-start(bf16[2432,128]{1,0:T(8,128)(2,1)S(1)} %shard_map.37), channel_id=1, source_target_pairs={{0,511},{1,2},{2,1},{3,4},{4,3},{5,6},{6,5},{7,8},{8,7},{9,10},{10... | collective-permute-start | bytes 1867784 | tf_op jit(solution)/shard_map/ppermute | solution.py:372
